TPU v7x, 128 devices: a whole 4x4x4 slice. The times are simulated.
128 devices in a mesh: region: 4 (over z), tile: 32 (over y, x, core).
Axes of the slice: x: 4, y: 4, z: 4, core: 2. Of those that a mesh axis runs over, the one named last changes fastest.
Arguments:
- jacobian: bfloat16 [40, 30, 262144], P(None, None, ('region', 'tile')), may hold values from -1 to 1
- misfit: float32 [40, 262144], P(None, ('region', 'tile'))
- model: float32 [30, 262144], P(None, ('region', 'tile')), may hold values from -0.15 to 0.15
- vertical_weight: float32 [29, 262144], P(None, ('region', 'tile')), may hold values from 0.2 to 2
- lateral_weight: float32 [64, 4096], P('region', 'tile'), may hold values from 0.2 to 2
- send_order: int32 [262144], P(('region', 'tile')), may hold values from 0 to 2047, as said below
- line_id: int32 [262144], P(('region', 'tile')), may hold values from 0 to 511, as said below
Outputs:
- new_model: float32 [30, 262144], P(None, ('region', 'tile'))
- line_profile: float32 [512, 30], P(('region', 'tile'))
Inputs may be any that keep to these rules, and one draw needn't show every extreme that they name: `send_order`: each aligned block of 2048 entries holds every number of 0 to 2047 once. `line_id`: let M = 128. Each aligned block b of 2048 entries is cut into 12 runs of one or more entries, in order; for k below 4, run k holds line b * 4 + k, run 4 + k holds line ((b - 1) mod M) * 4 + k, and run 2 * 4 + k holds line ((b - M / 2) mod M) * 4 + k.
All inputs are finite; a program needn't handle non-finite values.
Results may differ from a plain program's by a relative error of at most 0.0003.
Values sent between devices are 32-bit elements; how exact they have to be, the bound alone decides.
A program may use at most 64 MiB of HBM per device.

v0:
```python
import jax
import jax.numpy as jnp
from jax import lax
from jax.sharding import PartitionSpec as P

LINES_DEV = 4
ITERS = 2


damping = 0.05
neighbours = ((1, 0, 1.0), (-1, 0, 1.0), (0, 1, 0.5), (0, -1, 0.5))


def padded_2(array, sides, width):
    for axis, dim in sides:
        peers, length = (lax.axis_size(axis), array.shape[dim])
        up = [(i, (i + 1) % peers) for i in range(peers - 1)]
        down = [(j, i) for i, j in up]
        last = lax.slice_in_dim(array, length - width, length, axis=dim)
        first = lax.slice_in_dim(array, 0, width, axis=dim)
        before = lax.ppermute(last, axis, up)
        after = lax.ppermute(first, axis, down)
        array = jnp.concatenate([before, array, after], axis=dim)
    return array


def squared_norm(residual):
    return lax.psum(jnp.sum(residual * residual), ("region", "tile"))


def body(jacobian, misfit, model, vertical_weight, lateral_weight, send_order, line_id):
    layers, soundings = model.shape
    regions = lax.axis_size("region")
    tile_count = lax.axis_size("tile")
    devices = regions * tile_count
    per_peer = soundings // devices
    cells_along, cells_across = lateral_weight.shape
    positions = jnp.arange(soundings, dtype=jnp.int32)
    inverse = jnp.zeros((soundings,), jnp.int32).at[send_order].set(positions)
    right_side = jnp.sum(jacobian.astype(jnp.float32) * misfit[:, None, :], axis=0)
    update = jnp.zeros_like(right_side)
    residual = right_side
    direction = right_side
    norm_old = squared_norm(residual)
    for iteration in range(ITERS):
        predicted = jnp.sum(jacobian.astype(jnp.float32) * direction[None], axis=1)
        vertical_flux = vertical_weight * (direction[:-1] - direction[1:])
        local_sum = (
            jnp.sum(jacobian.astype(jnp.float32) * predicted[:, None, :], axis=0)
            + (jnp.pad(vertical_flux, ((0, 1), (0, 0))) - jnp.pad(vertical_flux, ((1, 0), (0, 0))))
            + damping * direction
        )
        ordered = jnp.take(direction, send_order, axis=1)
        to_arrived = lax.all_to_all(
            ordered.reshape(layers, devices, per_peer),
            ("region", "tile"),
            split_axis=1,
            concat_axis=1,
            tiled=True,
        )
        grid_field = to_arrived.reshape(layers, cells_along, cells_across)
        stacked = jnp.concatenate([grid_field, lateral_weight[None]], axis=0)
        padded = padded_2(stacked, (("region", 1), ("tile", 2)), 1)
        fields = padded[:-1]
        conduct = padded[-1]
        summed = jnp.zeros_like(grid_field)
        for step_row, step_col, factor in neighbours:
            beside = fields[
                :,
                1 + step_row : 1 + step_row + cells_along,
                1 + step_col : 1 + step_col + cells_across,
            ]
            beside_weight = conduct[
                1 + step_row : 1 + step_row + cells_along,
                1 + step_col : 1 + step_col + cells_across,
            ]
            summed = summed + 0.5 * factor * (lateral_weight + beside_weight) * (
                grid_field - beside
            )
        arrived = lax.all_to_all(
            summed.reshape(layers, devices, per_peer),
            ("region", "tile"),
            split_axis=1,
            concat_axis=1,
            tiled=True,
        )
        applied = local_sum + jnp.take(arrived.reshape(layers, soundings), inverse, axis=1)
        curvature = lax.psum(jnp.sum(direction * applied), ("region", "tile"))
        step_length = norm_old / curvature
        update = update + step_length * direction
        if iteration + 1 < ITERS:
            residual = residual - step_length * applied
            norm_new = squared_norm(residual)
            direction = residual + norm_new / norm_old * direction
            norm_old = norm_new
    new_model = model + update
    groups_all = LINES_DEV * devices
    line_sums = jax.ops.segment_sum(new_model.T, line_id, num_segments=groups_all)
    counts = jax.ops.segment_sum(
        jnp.ones((soundings,), jnp.float32), line_id, num_segments=groups_all
    )
    own_sums, own_counts = (
        lax.psum_scatter(line_sums, ("region", "tile"), scatter_dimension=0, tiled=True),
        lax.psum_scatter(counts, ("region", "tile"), scatter_dimension=0, tiled=True),
    )
    return (new_model, own_sums / own_counts[:, None])


def solution(mesh):
    in_specs = (
        P(None, None, ("region", "tile")),
        P(None, ("region", "tile")),
        P(None, ("region", "tile")),
        P(None, ("region", "tile")),
        P("region", "tile"),
        P(("region", "tile")),
        P(("region", "tile")),
    )
    out_specs = (P(None, ("region", "tile")), P(("region", "tile"), None))
    return jax.shard_map(body, mesh=mesh, in_specs=in_specs, out_specs=out_specs, check_vma=False)
```

profile of v0, /device:TPU:1, one launch (start us, length us, event | category | flops | bytes accessed | tf_op | source)
XLA Modules:
  0.0 475.3 jit_solution(4917216227684881199)
XLA Ops:
  0.6 1.3 compare_select_fusion.1
  1.9 0.7 compare_and_fusion.1
  2.6 3.8 fusion
  6.9 5.5 %gather_fusion = f32[2048,30]{1,0:T(8,128)S(1)} fusion(f32[30,2048]{0,1:T(8,128)S(1)} %copy.120, s32[2048]{0:T(1024)S(1)} %get-tuple-element.41), kind=kCustom, calls=%fused_computation.clone | custom fusion | bytes 499712 | tf_op jit(solution)/shard_map/jit(_take)/gather | solution.py:53
  12.7 2.2 reshape.132
  14.9 11.5 %all-to-all-start = ((f32[128,1,480]{2,1,0:T(1,128)}), f32[128,1,480]{2,1,0:T(1,128)S(1)}, u32[]{:S(2)}, u32[]{:S(2)}) async-start(f32[128,1,480]{2,1,0:T(1,128)} %reshape.132), calls=%async_computation | async-start | bytes 524288 | tf_op jit(solution)/shard_map/all_to_all | solution.py:54
  26.8 0.8 fusion.13
  27.5 4.3 fusion.1
  31.8 5.7 %all-to-all-done = f32[128,1,480]{2,1,0:T(1,128)S(1)} async-done(((f32[128,1,480]{2,1,0:T(1,128)}), f32[128,1,480]{2,1,0:T(1,128)S(1)}, u32[]{:S(2)}, u32[]{:S(2)}) %all-to-all-start) | async-done | bytes 245792 | tf_op jit(solution)/shard_map/all_to_all | solution.py:54
  37.9 1.2 reduce
  39.1 0.7 reshape.133
  39.8 0.8 fusion.30
  40.6 1.9 collective-permute-start
  42.5 1.3 collective-permute-start.1
  44.1 1.0 copy.123
  45.2 2.5 collective-permute-done.1
  47.7 1.0 pad_maximum_fusion.6
  48.7 0.9 fusion.46
  49.6 3.9 collective-permute-start.2
  53.6 1.9 collective-permute-start.3
  55.5 4.6 fusion.2
  60.1 8.7 %scatter_custom_fusion = s32[2048]{0:T(1024)} fusion(s32[2048]{0:T(1024)} %get-tuple-element.40, s32[2048]{0:T(1024)S(1)} %iota.3, s32[]{:T(128)} %constant.4.clone.1), kind=kCustom, calls=%fused_computation.119 | custom fusion | bytes 8704 | tf_op jit(solution)/shard_map/scatter | solution.py:39
  69.0 0.7 fusion.39
  69.6 1.1 pad_maximum_fusion.10
  70.7 1.3 copy.139
  72.0 2.3 copy.140
  74.3 4.3 fusion.9
  78.6 3.5 reshape.134
  82.1 7.5 %all-to-all-start.1 = ((f32[128,1,480]{2,1,0:T(1,128)}), f32[128,1,480]{2,1,0:T(1,128)S(1)}, u32[]{:S(2)}, u32[]{:S(2)}) async-start(f32[128,1,480]{2,1,0:T(1,128)} %reshape.134), calls=%async_computation.1 | async-start | bytes 524288 | tf_op jit(solution)/shard_map/all_to_all | solution.py:80
  89.6 0.7 compare_and_fusion
  90.3 0.7 fusion.40
  91.0 9.7 %all-to-all-done.1 = f32[128,1,480]{2,1,0:T(1,128)S(1)} async-done(((f32[128,1,480]{2,1,0:T(1,128)}), f32[128,1,480]{2,1,0:T(1,128)S(1)}, u32[]{:S(2)}, u32[]{:S(2)}) %all-to-all-start.1) | async-done | bytes 245792 | tf_op jit(solution)/shard_map/all_to_all | solution.py:80
  100.7 1.2 reduce.1
  101.9 0.7 reshape.135
  102.6 5.5 %gather_fusion.1 = f32[2048,30]{1,0:T(8,128)S(1)} fusion(f32[30,2048]{0,1:T(8,128)S(1)} %bitcast.40, s32[2048]{0:T(1024)S(1)} %fusion.40), kind=kCustom, calls=%fused_computation.1.clone | custom fusion | bytes 499712 | tf_op jit(solution)/shard_map/jit(_take)/gather | solution.py:87
  108.4 0.8 multiply_reduce_fusion.1
  109.2 62.9 %all-reduce.7 = (f32[]{:T(128)}, f32[]{:T(128)}) all-reduce(f32[]{:T(128)} %get-tuple-element.16, f32[]{:T(128)} %get-tuple-element.15), channel_id=1, replica_groups=mesh['region'=4,'tile'=32] {'region','tile'}, use_global_device_ids=true, to_apply=%region_2.0 | all-reduce | flops 2 | bytes 16 | tf_op jit(solution)/shard_map/psum | solution.py:28
  173.4 0.7 multiply_reduce_fusion
  174.1 62.8 %psum.30 = f32[]{:T(128)} all-reduce(f32[]{:T(128)} %multiply_reduce_fusion), channel_id=1, replica_groups=mesh['region'=4,'tile'=32] {'region','tile'}, use_global_device_ids=true, to_apply=%region_9.11 | all-reduce | flops 1 | bytes 8 | tf_op jit(solution)/shard_map/psum | solution.py:28
  238.6 5.5 %gather_fusion.2 = f32[2048,30]{1,0:T(8,128)S(1)} fusion(f32[30,2048]{0,1:T(8,128)S(1)} %copy.129, s32[2048]{0:T(1024)S(1)} %get-tuple-element.41), kind=kCustom, calls=%fused_computation.2.clone | custom fusion | bytes 499712 | tf_op jit(solution)/shard_map/jit(_take)/gather | solution.py:53
  244.5 2.2 reshape.136
  246.6 5.0 %all-to-all-start.2 = ((f32[128,1,480]{2,1,0:T(1,128)}), f32[128,1,480]{2,1,0:T(1,128)S(1)}, u32[]{:S(2)}, u32[]{:S(2)}) async-start(f32[128,1,480]{2,1,0:T(1,128)} %reshape.136), calls=%async_computation.2 | async-start | bytes 524288 | tf_op jit(solution)/shard_map/all_to_all | solution.py:54
  251.6 11.1 %all-to-all-done.2 = f32[128,1,480]{2,1,0:T(1,128)S(1)} async-done(((f32[128,1,480]{2,1,0:T(1,128)}), f32[128,1,480]{2,1,0:T(1,128)S(1)}, u32[]{:S(2)}, u32[]{:S(2)}) %all-to-all-start.2) | async-done | bytes 245792 | tf_op jit(solution)/shard_map/all_to_all | solution.py:54
  262.7 1.2 reduce.2
  263.9 0.7 reshape.137
  265.0 1.9 collective-permute-start.4
  266.9 1.3 collective-permute-start.5
  268.2 3.1 collective-permute-done.5
  271.6 3.9 collective-permute-start.6
  275.5 2.1 collective-permute-start.7
  277.6 3.6 fusion.3
  281.2 3.2 collective-permute-done.7
  285.4 2.2 reshape.138
  287.5 8.8 %all-to-all-start.3 = ((f32[128,1,480]{2,1,0:T(1,128)}), f32[128,1,480]{2,1,0:T(1,128)S(1)}, u32[]{:S(2)}, u32[]{:S(2)}) async-start(f32[128,1,480]{2,1,0:T(1,128)} %reshape.138), calls=%async_computation.3 | async-start | bytes 524288 | tf_op jit(solution)/shard_map/all_to_all | solution.py:80
  296.4 3.8 fusion.4
  300.2 7.2 %all-to-all-done.3 = f32[128,1,480]{2,1,0:T(1,128)S(1)} async-done(((f32[128,1,480]{2,1,0:T(1,128)}), f32[128,1,480]{2,1,0:T(1,128)S(1)}, u32[]{:S(2)}, u32[]{:S(2)}) %all-to-all-start.3) | async-done | bytes 245792 | tf_op jit(solution)/shard_map/all_to_all | solution.py:80
  307.4 1.2 reduce.3
  308.6 0.7 reshape.139
  309.3 5.5 %gather_fusion.3 = f32[2048,30]{1,0:T(8,128)S(1)} fusion(f32[30,2048]{0,1:T(8,128)S(1)} %bitcast.39, s32[2048]{0:T(1024)S(1)} %fusion.40), kind=kCustom, calls=%fused_computation.3.clone | custom fusion | bytes 499712 | tf_op jit(solution)/shard_map/jit(_take)/gather | solution.py:87
  315.1 0.7 fusion.15
  315.8 14.8 %scatter_custom_fusion.2 = f32[512]{0:T(512)S(1)} fusion(s32[2048]{0:T(1024)} %param.15, f32[2048]{0:T(1024)S(1)} %broadcast.41, f32[]{:T(128)} %constant.15.clone.1), kind=kCustom, calls=%fused_computation.122 | custom fusion | flops 2048 | bytes 2560 | tf_op jit(solution)/shard_map/scatter-add | solution.py:99
  330.6 62.9 %psum.31 = f32[]{:T(128)} all-reduce(f32[]{:T(128)} %fusion.15), channel_id=1, replica_groups=mesh['region'=4,'tile'=32] {'region','tile'}, use_global_device_ids=true, to_apply=%region_13.15 | all-reduce | flops 1 | bytes 8 | tf_op jit(solution)/shard_map/psum | solution.py:88
  395.2 14.8 %scatter_custom_fusion.1 = f32[512,30]{1,0:T(8,128)S(1)} fusion(s32[2048]{0:T(1024)} %param.15, f32[2048,30]{1,0:T(8,128)S(1)} %copy.137, f32[]{:T(128)} %constant.15.clone.1), kind=kCustom, calls=%fused_computation.80 | custom fusion | flops 61440 | bytes 61952 | tf_op jit(solution)/shard_map/scatter-add | solution.py:98
  410.1 64.5 %all-reduce.6 = (f32[512,30]{1,0:T(8,128)S(1)}, f32[512]{0:T(512)S(1)}) all-reduce(f32[512,30]{1,0:T(8,128)S(1)} %scatter_custom_fusion.1, f32[512]{0:T(512)S(1)} %scatter_custom_fusion.2), channel_id=2, replica_groups=mesh['region'=4,'tile'=32] {'region','tile'}, use_global_device_ids=true, to_apply=%region_15.17.clone | all-reduce | flops 15872 | bytes 126976
  (54 shorter events, 6.3 us)
Async XLA Ops:
  2.6 10.1 %copy-start.8 = (pred[2048]{0:T(1024)(128)(4,1)}, pred[2048]{0:T(1024)(128)(4,1)S(1)}, u32[]{:S(2)}) copy-start(pred[2048]{0:T(1024)(128)(4,1)S(1)} %compare_and_fusion.1) | copy-start | bytes 6148
  6.5 19.9 %copy-start.6 = (f32[16,128]{1,0:T(8,128)S(1)}, f32[16,128]{1,0:T(8,128)}, u32[]{:S(2)}) copy-start(f32[16,128]{1,0:T(8,128)} %param.13) | copy-start | bytes 24580
  6.5 20.3 %copy-start.2 = (f32[29,2048]{1,0:T(8,128)S(1)}, f32[29,2048]{1,0:T(8,128)}, u32[]{:S(2)}) copy-start(f32[29,2048]{1,0:T(8,128)} %param.12) | copy-start | bytes 712708
  14.9 22.6 %all-to-all-start = ((f32[128,1,480]{2,1,0:T(1,128)}), f32[128,1,480]{2,1,0:T(1,128)S(1)}, u32[]{:S(2)}, u32[]{:S(2)}) async-start(f32[128,1,480]{2,1,0:T(1,128)} %reshape.132), calls=%async_computation | async-start | bytes 524288 | tf_op jit(solution)/shard_map/all_to_all | solution.py:54
  40.6 4.6 collective-permute-start
  42.5 5.2 %collective-permute-start.1 = (f32[31,1,128]{0,2,1:T(8,128)}, f32[31,1,128]{0,2,1:T(8,128)S(1)}, u32[]{:S(2)}, u32[]{:S(2)}) collective-permute-start(f32[31,1,128]{0,2,1:T(8,128)} %get-tuple-element.22), channel_id=1, source_target_pairs={{32,0},{64,32},{96,64},{33,1},{65,33},{97,65},{34,2},{66,34},{98,6... | collective-permute-start | bytes 47624 | tf_op jit(solution)/shard_map/ppermute | solution.py:22
  45.1 23.7 %copy-start = (f32[31,16,128]{2,0,1:T(8,128)S(1)}, f32[31,16,128]{2,0,1:T(8,128)}, u32[]{:S(2)}) copy-start(f32[31,16,128]{2,0,1:T(8,128)} %copy.123) | copy-start | bytes 761860
  49.6 19.2 %collective-permute-start.2 = (f32[31,18,1]{2,0,1:T(8,128)}, f32[31,18,1]{2,0,1:T(8,128)S(1)}, u32[]{:S(2)}, u32[]{:S(2)}) collective-permute-start(f32[31,18,1]{2,0,1:T(8,128)} %get-tuple-element.29), channel_id=1, source_target_pairs={{0,1},{1,2},{2,3},{3,4},{4,5},{5,6},{6,7},{7,8},{8,9},{9,10},{10,1... | collective-permute-start | bytes 6704 | tf_op jit(solution)/shard_map/ppermute | solution.py:21
  53.6 15.2 %collective-permute-start.3 = (f32[31,18,1]{2,0,1:T(8,128)}, f32[31,18,1]{2,0,1:T(8,128)S(1)}, u32[]{:S(2)}, u32[]{:S(2)}) collective-permute-start(f32[31,18,1]{2,0,1:T(8,128)} %get-tuple-element.28), channel_id=1, source_target_pairs={{1,0},{2,1},{3,2},{4,3},{5,4},{6,5},{7,6},{8,7},{9,8},{10,9},{11,1... | collective-permute-start | bytes 6704 | tf_op jit(solution)/shard_map/ppermute | solution.py:22
  78.6 29.8 %copy-start.4 = (f32[29,2048]{1,0:T(8,128)S(1)}, f32[29,2048]{1,0:T(8,128)}, u32[]{:S(2)}) copy-start(f32[29,2048]{1,0:T(8,128)} %fusion.13) | copy-start | bytes 712708
  78.6 29.8 %copy-start.5 = (f32[30,2048]{1,0:T(8,128)S(1)}, f32[30,2048]{1,0:T(8,128)}, u32[]{:S(2)}) copy-start(f32[30,2048]{1,0:T(8,128)} %fusion.2) | copy-start | bytes 737284
  82.1 18.6 %all-to-all-start.1 = ((f32[128,1,480]{2,1,0:T(1,128)}), f32[128,1,480]{2,1,0:T(1,128)S(1)}, u32[]{:S(2)}, u32[]{:S(2)}) async-start(f32[128,1,480]{2,1,0:T(1,128)} %reshape.134), calls=%async_computation.1 | async-start | bytes 524288 | tf_op jit(solution)/shard_map/all_to_all | solution.py:80
  102.5 141.6 %copy-start.9 = (pred[2048]{0:T(1024)(128)(4,1)S(1)}, pred[2048]{0:T(1024)(128)(4,1)}, u32[]{:S(2)}) copy-start(pred[2048]{0:T(1024)(128)(4,1)} %copy-done.8) | copy-start | bytes 6148
  238.6 29.5 %copy-start.3 = (f32[29,2048]{1,0:T(8,128)S(1)}, f32[29,2048]{1,0:T(8,128)}, u32[]{:S(2)}) copy-start(f32[29,2048]{1,0:T(8,128)} %param.12) | copy-start | bytes 712708
  246.6 16.1 %all-to-all-start.2 = ((f32[128,1,480]{2,1,0:T(1,128)}), f32[128,1,480]{2,1,0:T(1,128)S(1)}, u32[]{:S(2)}, u32[]{:S(2)}) async-start(f32[128,1,480]{2,1,0:T(1,128)} %reshape.136), calls=%async_computation.2 | async-start | bytes 524288 | tf_op jit(solution)/shard_map/all_to_all | solution.py:54
  265.0 3.3 collective-permute-start.4
  266.9 4.5 collective-permute-start.5
  271.6 9.6 %collective-permute-start.6 = (f32[31,18,1]{2,1,0:T(8,128)S(1)}, f32[31,18,1]{2,1,0:T(8,128)S(1)}, u32[]{:S(2)}, u32[]{:S(2)}) collective-permute-start(f32[31,18,1]{2,1,0:T(8,128)S(1)} %get-tuple-element.25), channel_id=1, source_target_pairs={{0,1},{1,2},{2,3},{3,4},{4,5},{5,6},{6,7},{7,8},{8,9},{9,10},{10,1... | collective-permute-start | bytes 6704 | tf_op jit(solution)/shard_map/ppermute | solution.py:21
  275.5 9.0 %collective-permute-start.7 = (f32[31,18,1]{2,1,0:T(8,128)S(1)}, f32[31,18,1]{2,1,0:T(8,128)S(1)}, u32[]{:S(2)}, u32[]{:S(2)}) collective-permute-start(f32[31,18,1]{2,1,0:T(8,128)S(1)} %get-tuple-element.24), channel_id=1, source_target_pairs={{1,0},{2,1},{3,2},{4,3},{5,4},{6,5},{7,6},{8,7},{9,8},{10,9},{11,1... | collective-permute-start | bytes 6704 | tf_op jit(solution)/shard_map/ppermute | solution.py:22
  287.5 19.9 %all-to-all-start.3 = ((f32[128,1,480]{2,1,0:T(1,128)}), f32[128,1,480]{2,1,0:T(1,128)S(1)}, u32[]{:S(2)}, u32[]{:S(2)}) async-start(f32[128,1,480]{2,1,0:T(1,128)} %reshape.138), calls=%async_computation.3 | async-start | bytes 524288 | tf_op jit(solution)/shard_map/all_to_all | solution.py:80
  296.4 98.4 %copy-start.7 = (f32[30,2048]{1,0:T(8,128)S(1)}, f32[30,2048]{1,0:T(8,128)}, u32[]{:S(2)}) copy-start(f32[30,2048]{1,0:T(8,128)} %param.11) | copy-start | bytes 737284
  394.9 80.5 %copy-start.1 = (f32[30,2048]{1,0:T(8,128)}, f32[30,2048]{1,0:T(8,128)S(1)}, u32[]{:S(2)}) copy-start(f32[30,2048]{1,0:T(8,128)S(1)} %add_add_fusion) | copy-start | bytes 737284
where the time goes:
time: 477 us; the launch traced here: 475 us
  blocking collectives  253 us (53%)
  other arithmetic  71 us (15%)
  local copies, waits for them, and re-layouts  52.6 us (11%)
  starting transfers between devices  51 us (11%)
  waiting for transfers between devices  42.5 us (9%)
  between operations  5.07 us (1%)
    psum x2, blocking collectives, squared_norm(): return lax.psum(jnp.sum(residual * residual), ('region', 'tile'))  126 us
    unnamed x1, blocking collectives  64.5 us
    psum x1, blocking collectives, body(): curvature = lax.psum(jnp.sum(direction * applied), ('region', 'tile'))  62.9 us
    all_to_all x2, waiting for transfers between devices, body(): lax.all_to_all(summed.reshape(layers, devices, per_peer), ('region', 'til...  16.9 us
    all_to_all x2, waiting for transfers between devices, body(): lax.all_to_all(ordered.reshape(layers, devices, per_peer), ('region', 'ti...  16.8 us
    all_to_all x2, starting transfers between devices, body(): lax.all_to_all(ordered.reshape(layers, devices, per_peer), ('region', 'ti...  16.5 us
    unnamed x32, local copies, waits for them, and re-layouts  16.4 us
    all_to_all x2, starting transfers between devices, body(): lax.all_to_all(summed.reshape(layers, devices, per_peer), ('region', 'til...  16.3 us
  transfers between devices with their start and end apart: 12, of which 7 were waited for; matrix products, arithmetic and copies ran while one was open for 6% of the time, Pallas kernels for 0%

commit v1 on v0

v1 whole, which is shorter than its diff:
```python
import jax
import jax.numpy as jnp
from jax import lax
from jax.experimental import pallas as pl
from jax.experimental.pallas import tpu as pltpu
from jax.sharding import PartitionSpec as P

LINES_DEV = 4
DAMPING = 0.05
GATES = 40
LAYERS = 30
PADDED = 32
SOUNDINGS = 2048
REGIONS = 4
TILES = 32
DEVICES = REGIONS * TILES
ROWS = 16
LANES = 128
BLOCKS = SOUNDINGS // LANES
CHUNKS = 4
MESH = pl.DeviceIdType.MESH
F32 = jnp.float32


def lane_iota(shape):
    return lax.broadcasted_iota(jnp.int32, shape, 1)


def row_iota(shape):
    return lax.broadcasted_iota(jnp.int32, shape, 0)


def total(values):
    return jnp.sum(values, keepdims=True)


def swap_pieces(parts):
    parts = list(parts)
    piece = lane_iota((8, LANES)) // 16
    for bit in (4, 2, 1):
        low = (piece & bit) == 0
        for first in range(8):
            if first & bit:
                continue
            a, b = parts[first], parts[first + bit]
            b_up = pltpu.roll(b, bit * 16, 1)
            a_down = pltpu.roll(a, LANES - bit * 16, 1)
            parts[first] = jnp.where(low, a, b_up)
            parts[first + bit] = jnp.where(low, a_down, b)
    return parts


def pick(source, group, index):
    low = index & (LANES - 1)
    high = index // LANES
    out = None
    for q in range(BLOCKS):
        block = source[group * 8 : group * 8 + 8, q * LANES : (q + 1) * LANES]
        taken = jnp.take_along_axis(block, low, axis=1, mode="promise_in_bounds")
        out = taken if out is None else jnp.where(high == q, taken, out)
    return out


def kernel(
    jac_hbm, misfit, model, vertical, lateral, order, order_s, line,
    new_model, profile,
    jac, fields, vert, send_a, recv_a, grid, coef, c_grid, d_grid, edge, side,
    send_b, recv_b, back, resid, inverse, onehot, extended,
    sums_s, sums_r, part_s, part_r,
    jac_sem, ring_s, ring_r, halo_s, halo_r, sums_ss, sums_rs,
):
    region = lax.axis_index("region")
    tile = lax.axis_index("tile")
    me = region * TILES + tile

    def place(device):
        return (device // TILES, device % TILES)

    def chunk_copy(chunk):
        columns = pl.ds(chunk * (SOUNDINGS // CHUNKS), SOUNDINGS // CHUNKS)
        return pltpu.make_async_copy(
            jac_hbm.at[:, :, columns], jac.at[:, :, columns], jac_sem.at[chunk]
        )

    for chunk in range(CHUNKS):
        chunk_copy(chunk).start()

    barrier = pltpu.get_barrier_semaphore()

    def greet(i, carry):
        pl.semaphore_signal(
            barrier, inc=1, device_id=place((me + i) % DEVICES), device_id_type=MESH
        )
        return carry

    lax.fori_loop(1, DEVICES, greet, 0)

    fields[...] = jnp.zeros_like(fields)
    vert[...] = jnp.zeros_like(vert)
    vert[0 : LAYERS - 1, :] = vertical[...]

    def local_part(block, sums):
        @pl.when(block % (BLOCKS // CHUNKS) == 0)
        def _():
            chunk_copy(block // (BLOCKS // CHUNKS)).wait()

        at = pl.ds(pl.multiple_of(block * LANES, LANES), LANES)

        def gather_gates(group, acc):
            data = misfit[pl.ds(pl.multiple_of(group * 8, 8), 8), at]
            for d in range(8):
                acc = acc + jac[group * 8 + d, :, at].astype(F32) * data[d : d + 1]
            return acc

        right = lax.fori_loop(0, GATES // 8, gather_gates, jnp.zeros((LAYERS, LANES), F32))

        def normal_gate(d, acc):
            sens = jac[d, :, at].astype(F32)
            return acc + sens * jnp.sum(sens * right, axis=0, keepdims=True)

        normal = lax.fori_loop(0, GATES, normal_gate, jnp.zeros((LAYERS, LANES), F32), unroll=8)
        fields[0:LAYERS, at] = right
        fields[PADDED : PADDED + LAYERS, at] = normal
        p = fields[0:PADDED, at]
        flux = vert[:, at] * (p - pltpu.roll(p, PADDED - 1, 0))
        applied = fields[PADDED:, at] + DAMPING * p + (flux - pltpu.roll(flux, 1, 0))
        fields[PADDED:, at] = applied
        return sums[0] + p * p, sums[1] + p * applied

    zero = jnp.zeros((PADDED, LANES), F32)
    square_sum, local_sum = lax.fori_loop(0, BLOCKS, local_part, (zero, zero))

    pl.semaphore_wait(barrier, DEVICES - 1)

    def send_block(i, carry):
        block = (me // 8 + i) % BLOCKS
        index = jnp.broadcast_to(order[pl.ds(block, 1), :], (8, LANES))
        for j, message in enumerate(swap_pieces([pick(fields, s, index) for s in range(8)])):
            send_a[block * 8 + j] = message
        for n in range(8):
            peer = block * 8 + (me + n) % 8

            def post():
                pltpu.make_async_remote_copy(
                    src_ref=send_a.at[peer],
                    dst_ref=recv_a.at[me],
                    send_sem=ring_s.at[0],
                    recv_sem=ring_r.at[0],
                    device_id=place(peer),
                    device_id_type=MESH,
                ).start()

            if n == 0:
                pl.when(i > 0)(post)
            else:
                post()
        return carry

    lax.fori_loop(0, BLOCKS, send_block, 0)
    recv_a[me] = send_a[me]

    places = row_iota((BLOCKS, LANES)) * LANES + lane_iota((BLOCKS, LANES))

    def invert(q, found):
        return jnp.where(places == order_s[q], q, found)

    inverse[...] = lax.fori_loop(
        0, SOUNDINGS, invert, jnp.zeros((BLOCKS, LANES), jnp.int32), unroll=16
    )

    run = row_iota((24, LANES))
    shift = jnp.where(run < 8, 0, jnp.where(run < 16, DEVICES - 1, DEVICES // 2))
    owner = (me + shift) & (DEVICES - 1)
    wanted = jnp.where((run & 7) < LINES_DEV, owner * LINES_DEV + (run & 7), -1)
    for block in range(BLOCKS):
        hit = line[block : block + 1, :] == wanted
        onehot[:, block * LANES : (block + 1) * LANES] = jnp.where(hit, 1.0, 0.0)
    extended[...] = jnp.ones_like(extended)
    extended[0:LAYERS, :] = model[...]

    def line_sums(slot, values):
        found = lax.dot_general(
            onehot[...], values, (((1,), (1,)), ((), ())),
            precision=lax.Precision.HIGHEST, preferred_element_type=F32,
        )
        for g in range(3):
            sums_s[g, slot, :, 0:PADDED] = found[8 * g : 8 * g + 8, :]

    sums_s[...] = jnp.zeros_like(sums_s)
    line_sums(0, extended[...])
    line_sums(1, fields[0:PADDED, :])

    def wait_ring(k, buffer, sem):
        whole = buffer.at[pl.ds(0, DEVICES - 1)]
        pltpu.make_async_copy(whole, whole, sem.at[k]).wait()

    wait_ring(0, recv_a, ring_r)
    wait_ring(0, send_a, ring_s)

    def place_row(i, carry):
        rows = swap_pieces([recv_a[i * 8 + j] for j in range(8)])
        for s in range(8):
            grid[i + 1, s * 8 : s * 8 + 8, :] = rows[s]
        grid[i + 1, LAYERS : LAYERS + 1, :] = lateral[pl.ds(i, 1), :]
        return carry

    lax.fori_loop(0, ROWS, place_row, 0)

    lane = lane_iota((PADDED, LANES))
    layer = row_iota((PADDED, LANES))

    def halo_copies(phase):
        ch = pl.ds(phase * PADDED, PADDED)
        above = ((region + REGIONS - 1) % REGIONS, tile)
        below = ((region + 1) % REGIONS, tile)
        left = (region, (tile + TILES - 1) % TILES)
        right = (region, (tile + 1) % TILES)
        pairs = (
            (grid.at[1, ch], grid.at[ROWS + 1, ch], above),
            (grid.at[ROWS, ch], grid.at[0, ch], below),
            (edge.at[phase, 0], side.at[phase, 1], left),
            (edge.at[phase, 1], side.at[phase, 0], right),
        )
        return [
            pltpu.make_async_remote_copy(
                src_ref=src, dst_ref=dst,
                send_sem=halo_s.at[phase, n], recv_sem=halo_r.at[phase, n],
                device_id=device, device_id_type=MESH,
            )
            for n, (src, dst, device) in enumerate(pairs)
        ]

    def halo_start(phase):
        first = phase * PADDED
        west = jnp.zeros((PADDED, LANES), F32)
        east = jnp.zeros((PADDED, LANES), F32)
        for i in range(ROWS):
            row = grid[i + 1, first : first + PADDED, :]
            west = jnp.where(lane == i, row if i == 0 else pltpu.roll(row, i, 1), west)
            east = jnp.where(lane == i, pltpu.roll(row, i + 1, 1), east)
        edge[phase, 0] = west
        edge[phase, 1] = east
        copies = halo_copies(phase)
        for copy in copies:
            copy.start()
        return copies

    def halo_finish(phase, copies):
        for copy in copies:
            copy.wait()
        ch = slice(phase * PADDED, (phase + 1) * PADDED)

        @pl.when(region == 0)
        def _():
            grid[0, ch, :] = jnp.zeros((PADDED, LANES), F32)

        @pl.when(region == REGIONS - 1)
        def _():
            grid[ROWS + 1, ch, :] = jnp.zeros((PADDED, LANES), F32)

        @pl.when(tile == 0)
        def _():
            side[phase, 0] = jnp.zeros((PADDED, LANES), F32)

        @pl.when(tile == TILES - 1)
        def _():
            side[phase, 1] = jnp.zeros((PADDED, LANES), F32)

    def lateral_row(i, phase, west, east):
        ch = slice(phase * PADDED, (phase + 1) * PADDED)
        here = grid[i + 1, ch, :]
        up, down = grid[i, ch, :], grid[i + 2, ch, :]
        west_of = jnp.where(lane == 0, west, pltpu.roll(here, 1, 1))
        east_of = jnp.where(lane == LANES - 1, east, pltpu.roll(here, LANES - 1, 1))
        if phase == 0:
            own = here[LAYERS : LAYERS + 1]
            for n, (other, factor) in enumerate(
                ((up, 0.5), (down, 0.5), (west_of, 0.25), (east_of, 0.25))
            ):
                coef[i, n : n + 1, :] = factor * (own + other[LAYERS : LAYERS + 1])
        return (
            coef[i, 0:1, :] * (here - up)
            + coef[i, 1:2, :] * (here - down)
            + coef[i, 2:3, :] * (here - west_of)
            + coef[i, 3:4, :] * (here - east_of)
        )

    def lateral_part(phase, out):
        def step(i, carry):
            west, east, dots = carry
            value = lateral_row(i, phase, west, east)
            out[i] = value
            here = grid[i + 1, 0:PADDED, :]
            return pltpu.roll(west, LANES - 1, 1), pltpu.roll(east, LANES - 1, 1), dots + here * value

        first = (side[phase, 0], pltpu.roll(side[phase, 1], LANES - 1, 1), zero)
        return lax.fori_loop(0, ROWS, step, first)[2]

    copies = halo_start(0)
    halo_finish(0, copies)
    lateral_sum = lateral_part(0, c_grid)

    inside = layer < LAYERS
    curve_part = total(jnp.where(inside, lateral_sum + local_sum, 0.0))
    square_part = total(square_sum)

    upper = row_iota((8, LANES)) < 4
    sublane = row_iota((8, LANES))

    def send_pair(i, carry):
        pair = (me // 16 + i) % (ROWS // 2)
        parts = [None] * 8
        for k in range(4):
            a = c_grid[2 * pair, 8 * k : 8 * k + 8, :]
            b = c_grid[2 * pair + 1, 8 * k : 8 * k + 8, :]
            if k == 3:
                a = jnp.where(sublane == 6, curve_part, jnp.where(sublane == 7, square_part, a))
                b = jnp.where(sublane == 6, curve_part, jnp.where(sublane == 7, square_part, b))
            parts[k] = jnp.where(upper, a, pltpu.roll(b, 4, 0))
            parts[k + 4] = jnp.where(upper, pltpu.roll(a, 4, 0), b)
        for j, message in enumerate(swap_pieces(parts)):
            send_b[pair * 16 + j] = message[0:4]
            send_b[pair * 16 + 8 + j] = message[4:8]
        for n in range(16):
            peer = pair * 16 + (me + n) % 16

            def post():
                pltpu.make_async_remote_copy(
                    src_ref=send_b.at[peer],
                    dst_ref=recv_b.at[me],
                    send_sem=ring_s.at[1],
                    recv_sem=ring_r.at[1],
                    device_id=place(peer),
                    device_id_type=MESH,
                ).start()

            if n == 0:
                pl.when(i > 0)(post)
            else:
                post()
        return carry

    lax.fori_loop(0, ROWS // 2, send_pair, 0)
    recv_b[me] = send_b[me]

    def add_image(i, carry):
        grid[i + 1, PADDED:, :] = grid[i + 1, PADDED:, :] + c_grid[i]
        return carry

    lax.fori_loop(0, ROWS, add_image, 0)
    copies = halo_start(1)
    halo_finish(1, copies)
    lateral_part(1, d_grid)

    wait_ring(1, recv_b, ring_r)
    wait_ring(1, send_b, ring_s)

    def unpack_pair(pair, carried):
        words = [
            jnp.concatenate([recv_b[pair * 16 + j], recv_b[pair * 16 + 8 + j]], axis=0)
            for j in range(8)
        ]
        parts = swap_pieces(words)
        even = pl.ds(pl.multiple_of(pair * 2 * LANES, LANES), LANES)
        odd = pl.ds(pl.multiple_of(pair * 2 * LANES + LANES, LANES), LANES)
        for k in range(4):
            a = jnp.where(upper, parts[k], pltpu.roll(parts[k + 4], 4, 0))
            b = jnp.where(upper, pltpu.roll(parts[k], 4, 0), parts[k + 4])
            back[8 * k : 8 * k + 8, even] = a
            back[8 * k : 8 * k + 8, odd] = b
            if k == 3:
                carried = carried + a + b
        return carried

    carried = lax.fori_loop(0, BLOCKS // 2, unpack_pair, jnp.zeros((8, LANES), F32))
    curve = total(carried[6:7]) * (1.0 / 16)
    square = total(carried[7:8]) * (1.0 / 16)
    step_0 = square / curve

    def second_part(block, sums):
        at = pl.ds(pl.multiple_of(block * LANES, LANES), LANES)
        index = jnp.broadcast_to(inverse[pl.ds(block, 1), :], (8, LANES))
        taken = jnp.concatenate([pick(back, k, index) for k in range(4)], axis=0)
        applied = fields[PADDED:, at] + jnp.where(inside, taken, 0.0)
        r = fields[0:PADDED, at] - step_0 * applied
        resid[:, at] = r
        drop = r - pltpu.roll(r, PADDED - 1, 0)
        trimmed = resid[0:LAYERS, at]

        def gate(d, acc):
            predicted = jnp.sum(jac[d, :, at].astype(F32) * trimmed, axis=0, keepdims=True)
            return acc + predicted * predicted

        gates = lax.fori_loop(0, GATES, gate, jnp.zeros((1, LANES), F32), unroll=8)
        return (
            sums[0] + r * r,
            sums[1] + r * applied,
            sums[2] + vert[:, at] * (drop * drop) + DAMPING * (r * r),
            sums[3] + gates,
        )

    r_square, r_image, r_curve, r_gates = lax.fori_loop(
        0, BLOCKS, second_part, (zero, zero, zero, jnp.zeros((1, LANES), F32))
    )

    def grid_curve(i, acc):
        r = grid[i + 1, 0:PADDED, :] - step_0 * grid[i + 1, PADDED:, :]
        return acc + r * (c_grid[i] - step_0 * d_grid[i])

    r_lateral = lax.fori_loop(0, ROWS, grid_curve, zero)
    r_curve = total(jnp.where(inside, r_curve + r_lateral, 0.0)) + total(r_gates)

    row = lane_iota((1, LANES))
    part = jnp.where(
        row == 0, total(r_square), jnp.where(row == 1, total(r_image), r_curve)
    )
    part_s[0] = part
    part_r[me] = part

    def share(i, carry):
        pltpu.make_async_remote_copy(
            src_ref=part_s.at[0],
            dst_ref=part_r.at[me],
            send_sem=ring_s.at[2],
            recv_sem=ring_r.at[2],
            device_id=place((me + i) % DEVICES),
            device_id_type=MESH,
        ).start()
        return carry

    lax.fori_loop(1, DEVICES, share, 0)

    line_sums(2, resid[...])
    sums_copies = []
    for g, offset in ((1, DEVICES - 1), (2, DEVICES // 2)):
        copy = pltpu.make_async_remote_copy(
            src_ref=sums_s.at[g],
            dst_ref=sums_r.at[g - 1],
            send_sem=sums_ss.at[g - 1],
            recv_sem=sums_rs.at[g - 1],
            device_id=place((me + offset) % DEVICES),
            device_id_type=MESH,
        )
        copy.start()
        sums_copies.append(copy)

    wait_ring(2, part_r, ring_r)
    wait_ring(2, part_r, ring_s)
    for copy in sums_copies:
        copy.wait()

    sums = jnp.sum(part_r[...], axis=0)
    square_1, cross, curve_r = sums[:, 0:1], sums[:, 1:2], sums[:, 2:3]
    beta = square_1 / square
    curve_1 = curve_r + 2.0 * beta * cross + beta * beta * curve
    step_1 = square_1 / curve_1
    weight = step_0 + step_1 * beta
    new_model[...] = (
        model[...] + weight * fields[0:LAYERS, :] + step_1 * resid[0:LAYERS, :]
    )
    sums = [sums_s[0, n] + sums_r[0, n] + sums_r[1, n] for n in range(3)]
    count = sums[0][:, LAYERS : LAYERS + 1]
    means = (sums[0] + weight * sums[1] + step_1 * sums[2]) / count
    profile[...] = means[0:LINES_DEV, 0:LAYERS]


def body(jacobian, misfit, model, vertical_weight, lateral_weight, send_order, line_id):
    vmem = pl.BlockSpec(memory_space=pltpu.VMEM)
    smem = pl.BlockSpec(memory_space=pltpu.SMEM)
    dma = pltpu.SemaphoreType.DMA
    return pl.pallas_call(
        kernel,
        out_shape=(
            jax.ShapeDtypeStruct((LAYERS, SOUNDINGS), F32),
            jax.ShapeDtypeStruct((LINES_DEV, LAYERS), F32),
        ),
        in_specs=[pl.BlockSpec(memory_space=pl.ANY), vmem, vmem, vmem, vmem, vmem, smem, vmem],
        out_specs=(vmem, vmem),
        scratch_shapes=[
            pltpu.VMEM((GATES, LAYERS, SOUNDINGS), jnp.bfloat16),
            pltpu.VMEM((2 * PADDED, SOUNDINGS), F32),
            pltpu.VMEM((PADDED, SOUNDINGS), F32),
            pltpu.VMEM((DEVICES, 8, LANES), F32),
            pltpu.VMEM((DEVICES, 8, LANES), F32),
            pltpu.VMEM((ROWS + 2, 2 * PADDED, LANES), F32),
            pltpu.VMEM((ROWS, 8, LANES), F32),
            pltpu.VMEM((ROWS, PADDED, LANES), F32),
            pltpu.VMEM((ROWS, PADDED, LANES), F32),
            pltpu.VMEM((2, 2, PADDED, LANES), F32),
            pltpu.VMEM((2, 2, PADDED, LANES), F32),
            pltpu.VMEM((DEVICES, 4, LANES), F32),
            pltpu.VMEM((DEVICES, 4, LANES), F32),
            pltpu.VMEM((PADDED, SOUNDINGS), F32),
            pltpu.VMEM((PADDED, SOUNDINGS), F32),
            pltpu.VMEM((BLOCKS, LANES), jnp.int32),
            pltpu.VMEM((24, SOUNDINGS), F32),
            pltpu.VMEM((PADDED, SOUNDINGS), F32),
            pltpu.VMEM((3, 3, 8, LANES), F32),
            pltpu.VMEM((2, 3, 8, LANES), F32),
            pltpu.VMEM((1, 1, LANES), F32),
            pltpu.VMEM((DEVICES, 1, LANES), F32),
            dma((CHUNKS,)),
            dma((3,)),
            dma((3,)),
            dma((2, 4)),
            dma((2, 4)),
            dma((2,)),
            dma((2,)),
        ],
        compiler_params=pltpu.CompilerParams(
            collective_id=0, has_side_effects=True, vmem_limit_bytes=48 * 1024 * 1024
        ),
    )(
        jacobian,
        misfit,
        model,
        vertical_weight,
        lateral_weight,
        send_order.reshape(BLOCKS, LANES),
        send_order,
        line_id.reshape(BLOCKS, LANES),
    )


def solution(mesh):
    in_specs = (
        P(None, None, ("region", "tile")),
        P(None, ("region", "tile")),
        P(None, ("region", "tile")),
        P(None, ("region", "tile")),
        P("region", "tile"),
        P(("region", "tile")),
        P(("region", "tile")),
    )
    out_specs = (P(None, ("region", "tile")), P(("region", "tile"), None))
    return jax.shard_map(body, mesh=mesh, in_specs=in_specs, out_specs=out_specs, check_vma=False)
```

time: 477 us -> 68 us (0.14)
  blocking collectives: 253 us -> 0 us
  other arithmetic: 71 us -> 0 us
  Pallas kernels: 0 us -> 58.4 us
  starting transfers between devices: 51 us -> 0 us
  local copies, waits for them, and re-layouts: 52.6 us -> 8.78 us
  waiting for transfers between devices: 42.5 us -> 0 us
    psum x3 -> x0, blocking collectives: 189 us -> none  [the longest x2 126 us: squared_norm(): return lax.psum(jnp.sum(residual * residual), ('region', 'tile'))]
    unnamed x1 -> x0, blocking collectives: 64.5 us -> none
    pallas_call x0 -> x1, Pallas kernels: none -> 58.4 us  [body(): pl.pallas_call(kernel, out_shape=(jax.ShapeDtypeStruct((LAYERS, SOUNDINGS...]
    all_to_all x4 -> x0, waiting for transfers between devices: 33.7 us -> none  [the longest x2 16.9 us: body(): lax.all_to_all(summed.reshape(layers, devices, per_peer), ('region', 'til...]
    all_to_all x4 -> x0, starting transfers between devices: 32.8 us -> none  [the longest x2 16.5 us: body(): lax.all_to_all(ordered.reshape(layers, devices, per_peer), ('region', 'ti...]
    scatter-add x2 -> x0, other arithmetic: 29.6 us -> none  [the longest x1 14.8 us: body(): jax.ops.segment_sum(new_model.T, line_id, num_segments=groups_all)]
    gather x6 -> x0, local copies, waits for them, and re-layouts: 22.5 us -> none  [the longest x4 11.6 us: body(): jnp.take(arrived.reshape(layers, soundings), inverse, axis=1)]
    reduce_sum x8 -> x0, other arithmetic: 22.2 us -> none  [the longest x2 8.4 us: body(): jnp.sum(jacobian.astype(jnp.float32) * predicted[:, None, :], axis=0)]
  transfers between devices with their start and end apart: 12 -> 0, of which waited for: 7 -> 0; matrix products, arithmetic and copies ran while one was open for 6% -> 0% of each run, Pallas kernels for 0% -> 0%
where the time goes in v1:
time: 68 us; the launch traced here: 67.9 us
  Pallas kernels  58.4 us (86%)
  local copies, waits for them, and re-layouts  8.78 us (13%)
  between operations  0.72 us (1%)
    pallas_call x1, Pallas kernels, body(): pl.pallas_call(kernel, out_shape=(jax.ShapeDtypeStruct((LAYERS, SOUNDINGS...  58.4 us
    unnamed x15, local copies, waits for them, and re-layouts  8.78 us

profile of v1, /device:TPU:1, one launch (start us, length us, event | category | flops | bytes accessed | tf_op | source)
XLA Modules:
  0.0 67.9 jit_solution(1197001052301116545)
XLA Ops:
  0.6 0.0 copy-start.3
  0.6 0.0 copy-start.5
  0.7 0.0 copy-start.4
  0.7 0.0 copy-start.2
  0.7 0.0 copy-start.1
  0.7 0.0 copy-start
  0.7 7.5 %copy.9.jac_hbm = bf16[40,30,2048]{2,1,0:T(8,128)(2,1)} copy(bf16[40,30,2048]{2,0,1:T(8,128)(2,1)} %param.7) | data formatting | bytes 9830400 | tf_op args[0]
  8.2 0.0 copy-done.3
  8.2 0.0 copy-done.5
  8.2 0.0 copy-done.4
  8.2 0.0 copy-done.2
  8.2 0.0 copy-done.1
  8.2 0.0 copy-done
  8.2 58.4 %shard_map.86 = (f32[30,2048]{1,0:T(8,128)S(1)}, f32[4,30]{1,0:T(4,128)S(1)}) custom-call(bf16[40,30,2048]{2,1,0:T(8,128)(2,1)} %copy.9.jac_hbm, f32[40,2048]{1,0:T(8,128)S(1)} %copy-done, f32[30,2048]{1,0:T(8,128)S(1)} %copy-done.1, f32[29,2048]{1,0:T(8,128)S(1)} %copy-done.2, f32[16,128]{1,0:T(8,128)S(1)} %copy-done.4, s32[16,128]{1,0:T(8,128)S(1)} %bitcast.2, ...), custom_call_target="tpu_custom_call" | custom-call | tf_op jit(solution)/shard_map/pallas_call | solution.py:471
  66.6 0.7 %copy.12 = f32[30,2048]{1,0:T(8,128)} copy(f32[30,2048]{1,0:T(8,128)S(1)} %get-tuple-element.4) | data formatting | bytes 491520
  67.3 0.6 copy.13
Async XLA Ops:
  0.6 7.5 %copy-start.3 = (s32[2048]{0:T(1024)S(1)}, s32[2048]{0:T(1024)}, u32[]{:S(2)}) copy-start(s32[2048]{0:T(1024)} %order_s.1) | copy-start | bytes 24580
  0.6 7.5 %copy-start.5 = (s32[2048]{0:T(1024)S(1)}, s32[2048]{0:T(1024)}, u32[]{:S(2)}) copy-start(s32[2048]{0:T(1024)} %param.13) | copy-start | bytes 24580
  0.7 7.5 %copy-start.4 = (f32[16,128]{1,0:T(8,128)S(1)}, f32[16,128]{1,0:T(8,128)}, u32[]{:S(2)}) copy-start(f32[16,128]{1,0:T(8,128)} %lateral.1) | copy-start | bytes 24580
  0.7 7.5 %copy-start.2 = (f32[29,2048]{1,0:T(8,128)S(1)}, f32[29,2048]{1,0:T(8,128)}, u32[]{:S(2)}) copy-start(f32[29,2048]{1,0:T(8,128)} %vertical.1) | copy-start | bytes 712708
  0.7 7.5 %copy-start.1 = (f32[30,2048]{1,0:T(8,128)S(1)}, f32[30,2048]{1,0:T(8,128)}, u32[]{:S(2)}) copy-start(f32[30,2048]{1,0:T(8,128)} %model.1) | copy-start | bytes 737284
  0.7 7.5 %copy-start = (f32[40,2048]{1,0:T(8,128)S(1)}, f32[40,2048]{1,0:T(8,128)}, u32[]{:S(2)}) copy-start(f32[40,2048]{1,0:T(8,128)} %misfit.1) | copy-start | bytes 983044

commit v2 on v1

--- a/solution.py
+++ b/solution.py
@@ -18,7 +18,7 @@
 LANES = 128
 BLOCKS = SOUNDINGS // LANES
 CHUNKS = 4
-MESH = pl.DeviceIdType.MESH
+LOGICAL = pl.DeviceIdType.LOGICAL
 F32 = jnp.float32
 
 
@@ -50,6 +50,28 @@
     return parts
 
 
+def layers_of(group):
+    return range(8 * group, min(8 * group + 8, LAYERS))
+
+
+def fold_layers(terms):
+    parts = []
+    for term in terms:
+        rows = [term[8 * n : 8 * n + 8] for n in range(GATES // 8)]
+        while len(rows) > 1:
+            rows = [sum(rows[n : n + 2][1:], rows[n]) for n in range(0, len(rows), 2)]
+        parts.append(rows[0])
+    parts += [jnp.zeros((8, LANES), F32)] * (8 - len(parts))
+    row = row_iota((8, LANES))
+    for bit in (1, 2, 4):
+        low = (row & bit) == 0
+        parts = [
+            jnp.where(low, a, b) + pltpu.roll(jnp.where(low, b, a), bit, 0)
+            for a, b in zip(parts[::2], parts[1::2])
+        ]
+    return parts[0]
+
+
 def pick(source, group, index):
     low = index & (LANES - 1)
     high = index // LANES
@@ -62,42 +84,62 @@
 
 
 def kernel(
-    jac_hbm, misfit, model, vertical, lateral, order, order_s, line,
+    jac_in, misfit_in, model_in, vertical_in, lateral_in, order_in, order_flat, line_in,
     new_model, profile,
-    jac, fields, vert, send_a, recv_a, grid, coef, c_grid, d_grid, edge, side,
+    misfit, model, vertical, lateral, order, order_s, line,
+    jac, fields, vert, ordered, send_a, recv_a, grid, coef, c_grid, d_grid, edge, side,
     send_b, recv_b, back, resid, inverse, onehot, extended,
     sums_s, sums_r, part_s, part_r,
-    jac_sem, ring_s, ring_r, halo_s, halo_r, sums_ss, sums_rs,
+    in_sem, jac_sem, ring_s, ring_r, halo_s, halo_r, sums_ss, sums_rs,
 ):
     region = lax.axis_index("region")
     tile = lax.axis_index("tile")
     me = region * TILES + tile
 
     def place(device):
-        return (device // TILES, device % TILES)
+        return device
 
     def chunk_copy(chunk):
         columns = pl.ds(chunk * (SOUNDINGS // CHUNKS), SOUNDINGS // CHUNKS)
         return pltpu.make_async_copy(
-            jac_hbm.at[:, :, columns], jac.at[:, :, columns], jac_sem.at[chunk]
-        )
-
-    for chunk in range(CHUNKS):
+            jac_in.at[:, :, columns], jac.at[:, :, columns], jac_sem.at[chunk]
+        )
+
+    loads = [
+        pltpu.make_async_copy(src, dst, in_sem.at[n])
+        for n, (src, dst) in enumerate(
+            (
+                (misfit_in, misfit),
+                (vertical_in, vertical),
+                (order_in, order),
+                (order_flat, order_s),
+                (lateral_in, lateral),
+                (model_in, model),
+                (line_in, line),
+            )
+        )
+    ]
+    vert[PADDED - 8 :, :] = jnp.zeros((8, SOUNDINGS), F32)
+    chunk_copy(0).start()
+    loads[0].start()
+    loads[1].start()
+    for chunk in range(1, CHUNKS):
         chunk_copy(chunk).start()
+    for load in loads[2:]:
+        load.start()
 
     barrier = pltpu.get_barrier_semaphore()
 
     def greet(i, carry):
         pl.semaphore_signal(
-            barrier, inc=1, device_id=place((me + i) % DEVICES), device_id_type=MESH
+            barrier, inc=1, device_id=place((me + i) % DEVICES), device_id_type=LOGICAL
         )
         return carry
 
     lax.fori_loop(1, DEVICES, greet, 0)
 
-    fields[...] = jnp.zeros_like(fields)
-    vert[...] = jnp.zeros_like(vert)
-    vert[0 : LAYERS - 1, :] = vertical[...]
+    loads[0].wait()
+    loads[1].wait()
 
     def local_part(block, sums):
         @pl.when(block % (BLOCKS // CHUNKS) == 0)
@@ -106,21 +148,19 @@
 
         at = pl.ds(pl.multiple_of(block * LANES, LANES), LANES)
 
-        def gather_gates(group, acc):
-            data = misfit[pl.ds(pl.multiple_of(group * 8, 8), 8), at]
-            for d in range(8):
-                acc = acc + jac[group * 8 + d, :, at].astype(F32) * data[d : d + 1]
-            return acc
-
-        right = lax.fori_loop(0, GATES // 8, gather_gates, jnp.zeros((LAYERS, LANES), F32))
-
-        def normal_gate(d, acc):
-            sens = jac[d, :, at].astype(F32)
-            return acc + sens * jnp.sum(sens * right, axis=0, keepdims=True)
-
-        normal = lax.fori_loop(0, GATES, normal_gate, jnp.zeros((LAYERS, LANES), F32), unroll=8)
-        fields[0:LAYERS, at] = right
-        fields[PADDED : PADDED + LAYERS, at] = normal
+        gate_rows = misfit[:, at]
+        for group in range(PADDED // 8):
+            fields[8 * group : 8 * group + 8, at] = fold_layers(
+                [jac[l, :, at].astype(F32) * gate_rows for l in layers_of(group)]
+            )
+        predicted = jnp.zeros((GATES, LANES), F32)
+        for l in range(LAYERS):
+            predicted = predicted + jac[l, :, at].astype(F32) * fields[l : l + 1, at]
+        for group in range(PADDED // 8):
+            fields[PADDED + 8 * group : PADDED + 8 * group + 8, at] = fold_layers(
+                [jac[l, :, at].astype(F32) * predicted for l in layers_of(group)]
+            )
+        vert[0 : LAYERS - 1, at] = vertical[:, at]
         p = fields[0:PADDED, at]
         flux = vert[:, at] * (p - pltpu.roll(p, PADDED - 1, 0))
         applied = fields[PADDED:, at] + DAMPING * p + (flux - pltpu.roll(flux, 1, 0))
@@ -130,33 +170,44 @@
     zero = jnp.zeros((PADDED, LANES), F32)
     square_sum, local_sum = lax.fori_loop(0, BLOCKS, local_part, (zero, zero))
 
+    for load in loads[2:]:
+        load.wait()
     pl.semaphore_wait(barrier, DEVICES - 1)
 
-    def send_block(i, carry):
-        block = (me // 8 + i) % BLOCKS
-        index = jnp.broadcast_to(order[pl.ds(block, 1), :], (8, LANES))
-        for j, message in enumerate(swap_pieces([pick(fields, s, index) for s in range(8)])):
-            send_a[block * 8 + j] = message
-        for n in range(8):
-            peer = block * 8 + (me + n) % 8
-
-            def post():
-                pltpu.make_async_remote_copy(
-                    src_ref=send_a.at[peer],
-                    dst_ref=recv_a.at[me],
-                    send_sem=ring_s.at[0],
-                    recv_sem=ring_r.at[0],
-                    device_id=place(peer),
-                    device_id_type=MESH,
-                ).start()
-
-            if n == 0:
-                pl.when(i > 0)(post)
-            else:
-                post()
+    def send_group(i, carry):
+        first = (me // 32 + i) % 4 * 4
+
+        def order_block(n, c):
+            index = jnp.broadcast_to(order[pl.ds(first + n, 1), :], (8, LANES))
+            for k in range(8):
+                ordered[n, k] = pick(fields, k, index)
+            return c
+
+        lax.fori_loop(0, 4, order_block, 0, unroll=4)
+
+        def turn_block(n, c):
+            for j, message in enumerate(swap_pieces([ordered[n, k] for k in range(8)])):
+                send_a[(first + n) * 8 + j] = message
+            return c
+
+        lax.fori_loop(0, 4, turn_block, 0, unroll=4)
+
+        def post(n, c):
+            peer = first * 8 + (me + n) % 32
+            pltpu.make_async_remote_copy(
+                src_ref=send_a.at[peer],
+                dst_ref=recv_a.at[me],
+                send_sem=ring_s.at[0],
+                recv_sem=ring_r.at[0],
+                device_id=place(peer),
+                device_id_type=LOGICAL,
+            ).start()
+            return c
+
+        lax.fori_loop(jnp.where(i == 0, 1, 0), 32, post, 0)
         return carry
 
-    lax.fori_loop(0, BLOCKS, send_block, 0)
+    lax.fori_loop(0, 4, send_group, 0)
     recv_a[me] = send_a[me]
 
     places = row_iota((BLOCKS, LANES)) * LANES + lane_iota((BLOCKS, LANES))
@@ -204,17 +255,17 @@
         grid[i + 1, LAYERS : LAYERS + 1, :] = lateral[pl.ds(i, 1), :]
         return carry
 
-    lax.fori_loop(0, ROWS, place_row, 0)
+    lax.fori_loop(0, ROWS, place_row, 0, unroll=4)
 
     lane = lane_iota((PADDED, LANES))
     layer = row_iota((PADDED, LANES))
 
     def halo_copies(phase):
         ch = pl.ds(phase * PADDED, PADDED)
-        above = ((region + REGIONS - 1) % REGIONS, tile)
-        below = ((region + 1) % REGIONS, tile)
-        left = (region, (tile + TILES - 1) % TILES)
-        right = (region, (tile + 1) % TILES)
+        above = (region + REGIONS - 1) % REGIONS * TILES + tile
+        below = (region + 1) % REGIONS * TILES + tile
+        left = region * TILES + (tile + TILES - 1) % TILES
+        right = region * TILES + (tile + 1) % TILES
         pairs = (
             (grid.at[1, ch], grid.at[ROWS + 1, ch], above),
             (grid.at[ROWS, ch], grid.at[0, ch], below),
@@ -225,7 +276,7 @@
             pltpu.make_async_remote_copy(
                 src_ref=src, dst_ref=dst,
                 send_sem=halo_s.at[phase, n], recv_sem=halo_r.at[phase, n],
-                device_id=device, device_id_type=MESH,
+                device_id=device, device_id_type=LOGICAL,
             )
             for n, (src, dst, device) in enumerate(pairs)
         ]
@@ -286,15 +337,15 @@
         )
 
     def lateral_part(phase, out):
-        def step(i, carry):
-            west, east, dots = carry
-            value = lateral_row(i, phase, west, east)
+        west, east = side[phase, 0], side[phase, 1]
+        dots = [zero] * 2
+        for i in range(ROWS):
+            west_i = west if i == 0 else pltpu.roll(west, LANES - i, 1)
+            value = lateral_row(i, phase, west_i, pltpu.roll(east, LANES - 1 - i, 1))
             out[i] = value
-            here = grid[i + 1, 0:PADDED, :]
-            return pltpu.roll(west, LANES - 1, 1), pltpu.roll(east, LANES - 1, 1), dots + here * value
-
-        first = (side[phase, 0], pltpu.roll(side[phase, 1], LANES - 1, 1), zero)
-        return lax.fori_loop(0, ROWS, step, first)[2]
+            if phase == 0:
+                dots[i % 2] = dots[i % 2] + grid[i + 1, 0:PADDED, :] * value
+        return dots[0] + dots[1]
 
     copies = halo_start(0)
     halo_finish(0, copies)
@@ -307,8 +358,7 @@
     upper = row_iota((8, LANES)) < 4
     sublane = row_iota((8, LANES))
 
-    def send_pair(i, carry):
-        pair = (me // 16 + i) % (ROWS // 2)
+    def turn_pair(pair):
         parts = [None] * 8
         for k in range(4):
             a = c_grid[2 * pair, 8 * k : 8 * k + 8, :]
@@ -321,33 +371,39 @@
         for j, message in enumerate(swap_pieces(parts)):
             send_b[pair * 16 + j] = message[0:4]
             send_b[pair * 16 + 8 + j] = message[4:8]
-        for n in range(16):
-            peer = pair * 16 + (me + n) % 16
-
-            def post():
-                pltpu.make_async_remote_copy(
-                    src_ref=send_b.at[peer],
-                    dst_ref=recv_b.at[me],
-                    send_sem=ring_s.at[1],
-                    recv_sem=ring_r.at[1],
-                    device_id=place(peer),
-                    device_id_type=MESH,
-                ).start()
-
-            if n == 0:
-                pl.when(i > 0)(post)
-            else:
-                post()
+
+    def send_half(i, carry):
+        first = (me // 64 + i) % 2 * 4
+
+        def turn(n, c):
+            turn_pair(first + n)
+            return c
+
+        lax.fori_loop(0, 4, turn, 0, unroll=4)
+
+        def post(n, c):
+            peer = first * 16 + (me + n) % 64
+            pltpu.make_async_remote_copy(
+                src_ref=send_b.at[peer],
+                dst_ref=recv_b.at[me],
+                send_sem=ring_s.at[1],
+                recv_sem=ring_r.at[1],
+                device_id=place(peer),
+                device_id_type=LOGICAL,
+            ).start()
+            return c
+
+        lax.fori_loop(jnp.where(i == 0, 1, 0), 64, post, 0)
         return carry
 
-    lax.fori_loop(0, ROWS // 2, send_pair, 0)
+    lax.fori_loop(0, 2, send_half, 0)
     recv_b[me] = send_b[me]
 
     def add_image(i, carry):
         grid[i + 1, PADDED:, :] = grid[i + 1, PADDED:, :] + c_grid[i]
         return carry
 
-    lax.fori_loop(0, ROWS, add_image, 0)
+    lax.fori_loop(0, ROWS, add_image, 0, unroll=4)
     copies = halo_start(1)
     halo_finish(1, copies)
     lateral_part(1, d_grid)
@@ -372,7 +428,7 @@
                 carried = carried + a + b
         return carried
 
-    carried = lax.fori_loop(0, BLOCKS // 2, unpack_pair, jnp.zeros((8, LANES), F32))
+    carried = lax.fori_loop(0, BLOCKS // 2, unpack_pair, jnp.zeros((8, LANES), F32), unroll=4)
     curve = total(carried[6:7]) * (1.0 / 16)
     square = total(carried[7:8]) * (1.0 / 16)
     step_0 = square / curve
@@ -385,35 +441,41 @@
         r = fields[0:PADDED, at] - step_0 * applied
         resid[:, at] = r
         drop = r - pltpu.roll(r, PADDED - 1, 0)
-        trimmed = resid[0:LAYERS, at]
-
-        def gate(d, acc):
-            predicted = jnp.sum(jac[d, :, at].astype(F32) * trimmed, axis=0, keepdims=True)
-            return acc + predicted * predicted
-
-        gates = lax.fori_loop(0, GATES, gate, jnp.zeros((1, LANES), F32), unroll=8)
+        predicted = jnp.zeros((GATES, LANES), F32)
+        for l in range(LAYERS):
+            predicted = predicted + jac[l, :, at].astype(F32) * resid[l : l + 1, at]
         return (
             sums[0] + r * r,
             sums[1] + r * applied,
             sums[2] + vert[:, at] * (drop * drop) + DAMPING * (r * r),
-            sums[3] + gates,
+            sums[3] + predicted * predicted,
         )
 
     r_square, r_image, r_curve, r_gates = lax.fori_loop(
-        0, BLOCKS, second_part, (zero, zero, zero, jnp.zeros((1, LANES), F32))
+        0, BLOCKS, second_part, (zero, zero, zero, jnp.zeros((GATES, LANES), F32))
     )
 
     def grid_curve(i, acc):
         r = grid[i + 1, 0:PADDED, :] - step_0 * grid[i + 1, PADDED:, :]
         return acc + r * (c_grid[i] - step_0 * d_grid[i])
 
-    r_lateral = lax.fori_loop(0, ROWS, grid_curve, zero)
-    r_curve = total(jnp.where(inside, r_curve + r_lateral, 0.0)) + total(r_gates)
-
-    row = lane_iota((1, LANES))
-    part = jnp.where(
-        row == 0, total(r_square), jnp.where(row == 1, total(r_image), r_curve)
+    r_lateral = lax.fori_loop(0, ROWS, grid_curve, zero, unroll=4)
+    r_curve = jnp.where(inside, r_curve + r_lateral, 0.0)
+
+    def rows_sum(values):
+        return jnp.sum(values, axis=0, keepdims=True)
+
+    scalars = jnp.where(
+        sublane == 0,
+        rows_sum(r_square),
+        jnp.where(
+            sublane == 1,
+            rows_sum(r_image),
+            jnp.where(sublane == 2, rows_sum(r_curve) + rows_sum(r_gates), 0.0),
+        ),
     )
+    scalars = jnp.sum(scalars, axis=1, keepdims=True)
+    part = rows_sum(jnp.where(sublane == lane_iota((8, LANES)), scalars, 0.0))
     part_s[0] = part
     part_r[me] = part
 
@@ -424,7 +486,7 @@
             send_sem=ring_s.at[2],
             recv_sem=ring_r.at[2],
             device_id=place((me + i) % DEVICES),
-            device_id_type=MESH,
+            device_id_type=LOGICAL,
         ).start()
         return carry
 
@@ -439,7 +501,7 @@
             send_sem=sums_ss.at[g - 1],
             recv_sem=sums_rs.at[g - 1],
             device_id=place((me + offset) % DEVICES),
-            device_id_type=MESH,
+            device_id_type=LOGICAL,
         )
         copy.start()
         sums_copies.append(copy)
@@ -466,7 +528,6 @@
 
 def body(jacobian, misfit, model, vertical_weight, lateral_weight, send_order, line_id):
     vmem = pl.BlockSpec(memory_space=pltpu.VMEM)
-    smem = pl.BlockSpec(memory_space=pltpu.SMEM)
     dma = pltpu.SemaphoreType.DMA
     return pl.pallas_call(
         kernel,
@@ -474,12 +535,20 @@
             jax.ShapeDtypeStruct((LAYERS, SOUNDINGS), F32),
             jax.ShapeDtypeStruct((LINES_DEV, LAYERS), F32),
         ),
-        in_specs=[pl.BlockSpec(memory_space=pl.ANY), vmem, vmem, vmem, vmem, vmem, smem, vmem],
+        in_specs=[pl.BlockSpec(memory_space=pltpu.HBM)] * 8,
         out_specs=(vmem, vmem),
         scratch_shapes=[
-            pltpu.VMEM((GATES, LAYERS, SOUNDINGS), jnp.bfloat16),
+            pltpu.VMEM((GATES, SOUNDINGS), F32),
+            pltpu.VMEM((LAYERS, SOUNDINGS), F32),
+            pltpu.VMEM((LAYERS - 1, SOUNDINGS), F32),
+            pltpu.VMEM((ROWS, LANES), F32),
+            pltpu.VMEM((BLOCKS, LANES), jnp.int32),
+            pltpu.SMEM((SOUNDINGS,), jnp.int32),
+            pltpu.VMEM((BLOCKS, LANES), jnp.int32),
+            pltpu.VMEM((LAYERS, GATES, SOUNDINGS), jnp.bfloat16),
             pltpu.VMEM((2 * PADDED, SOUNDINGS), F32),
             pltpu.VMEM((PADDED, SOUNDINGS), F32),
+            pltpu.VMEM((4, 8, 8, LANES), F32),
             pltpu.VMEM((DEVICES, 8, LANES), F32),
             pltpu.VMEM((DEVICES, 8, LANES), F32),
             pltpu.VMEM((ROWS + 2, 2 * PADDED, LANES), F32),
@@ -499,6 +568,7 @@
             pltpu.VMEM((2, 3, 8, LANES), F32),
             pltpu.VMEM((1, 1, LANES), F32),
             pltpu.VMEM((DEVICES, 1, LANES), F32),
+            dma((7,)),
             dma((CHUNKS,)),
             dma((3,)),
             dma((3,)),
@@ -508,10 +578,10 @@
             dma((2,)),
         ],
         compiler_params=pltpu.CompilerParams(
-            collective_id=0, has_side_effects=True, vmem_limit_bytes=48 * 1024 * 1024
+            collective_id=0, has_side_effects=True, vmem_limit_bytes=63 * 1024 * 1024
         ),
     )(
-        jacobian,
+        jacobian.transpose(1, 0, 2),
         misfit,
         model,
         vertical_weight,

time: 68 us -> 51 us (0.75)
  Pallas kernels: 58.4 us -> 47.3 us
  local copies, waits for them, and re-layouts: 8.78 us -> 2.92 us
    pallas_call x1, Pallas kernels: 58.4 us -> 47.3 us  [body(): pl.pallas_call(kernel, out_shape=(jax.ShapeDtypeStruct((LAYERS, SOUNDINGS...]
    unnamed x15 -> x2, local copies, waits for them, and re-layouts: 8.78 us -> 2.92 us
where the time goes in v2:
time: 51 us; the launch traced here: 50.8 us
  Pallas kernels  47.3 us (93%)
  local copies, waits for them, and re-layouts  2.92 us (6%)
  between operations  0.64 us (1%)
    pallas_call x1, Pallas kernels, body(): pl.pallas_call(kernel, out_shape=(jax.ShapeDtypeStruct((LAYERS, SOUNDINGS...  47.3 us
    unnamed x2, local copies, waits for them, and re-layouts  2.92 us

profile of v2, /device:TPU:1, one launch (start us, length us, event | category | flops | bytes accessed | tf_op | source)
XLA Modules:
  0.0 50.8 jit_solution(971227854438316746)
XLA Ops:
  0.6 47.3 %shard_map.86 = (f32[30,2048]{1,0:T(8,128)}, f32[4,30]{1,0:T(4,128)}) custom-call(bf16[30,40,2048]{2,1,0:T(8,128)(2,1)} %bitcast.3, f32[40,2048]{1,0:T(8,128)} %misfit_in.1, f32[30,2048]{1,0:T(8,128)} %model_in.1, f32[29,2048]{1,0:T(8,128)} %vertical_in.1, f32[16,128]{1,0:T(8,128)} %lateral_in.1, s32[16,128]{1,0:T(8,128)} %bitcast.4, s32[2048]{0:T(1024)} %order_flat.1, ...), custom_call_target="tpu_custom_call" | custom-call | tf_op jit(solution)/shard_map/pallas_call | solution.py:532
  47.9 1.7 %copy.11 = f32[30,2048]{1,0:T(8,128)} copy(f32[30,2048]{1,0:T(8,128)} %get-tuple-element.4) | data formatting | bytes 491520
  49.6 1.2 %copy.12 = f32[4,30]{1,0:T(4,128)} copy(f32[4,30]{1,0:T(4,128)} %get-tuple-element.5) | data formatting | bytes 960

commit v3 on v2

--- a/solution.py
+++ b/solution.py
@@ -87,7 +87,7 @@
     jac_in, misfit_in, model_in, vertical_in, lateral_in, order_in, order_flat, line_in,
     new_model, profile,
     misfit, model, vertical, lateral, order, order_s, line,
-    jac, fields, vert, ordered, send_a, recv_a, grid, coef, c_grid, d_grid, edge, side,
+    jac, fields, vert, ordered, send_p, recv_p, send_l, recv_l, grid, coef, c_grid, d_grid, edge, side,
     send_b, recv_b, back, resid, inverse, onehot, extended,
     sums_s, sums_r, part_s, part_r,
     in_sem, jac_sem, ring_s, ring_r, halo_s, halo_r, sums_ss, sums_rs,
@@ -172,95 +172,124 @@
 
     for load in loads[2:]:
         load.wait()
+
+    upper = row_iota((8, LANES)) < 4
+    sublane = row_iota((8, LANES))
+    lane = lane_iota((PADDED, LANES))
+    layer = row_iota((PADDED, LANES))
+    inside = layer < LAYERS
+    quarter_row = row_iota((4, LANES))
+    quarter_lane = lane_iota((4, LANES))
+
+    def pack_pair(pair, a, b, buffer):
+        parts = [jnp.where(upper, a[k], pltpu.roll(b[k], 4, 0)) for k in range(4)]
+        parts += [jnp.where(upper, pltpu.roll(a[k], 4, 0), b[k]) for k in range(4)]
+        for j, message in enumerate(swap_pieces(parts)):
+            buffer[pair * 16 + j] = message[0:4]
+            buffer[pair * 16 + 8 + j] = message[4:8]
+
+    def unpack_pair(pair, buffer):
+        parts = swap_pieces(
+            [
+                jnp.concatenate([buffer[pair * 16 + j], buffer[pair * 16 + 8 + j]], axis=0)
+                for j in range(8)
+            ]
+        )
+        a = [jnp.where(upper, parts[k], pltpu.roll(parts[k + 4], 4, 0)) for k in range(4)]
+        b = [jnp.where(upper, pltpu.roll(parts[k], 4, 0), parts[k + 4]) for k in range(4)]
+        return a, b
+
+    def post(ring, source, target, peer):
+        pltpu.make_async_remote_copy(
+            src_ref=source.at[peer],
+            dst_ref=target.at[me],
+            send_sem=ring_s.at[ring],
+            recv_sem=ring_r.at[ring],
+            device_id=peer,
+            device_id_type=LOGICAL,
+        ).start()
+
+    def wait_ring(ring, buffer, sem):
+        whole = buffer.at[pl.ds(0, DEVICES - 1)]
+        pltpu.make_async_copy(whole, whole, sem.at[ring]).wait()
+
+    def edge_of(message, side_of):
+        out = jnp.zeros((4, LANES), F32)
+        for i in range(ROWS):
+            moved = pltpu.roll(message(i), (i - 15 * side_of) % LANES, 1)
+            out = jnp.where(quarter_lane % 16 == i, moved, out)
+        return out
+
+    def weight_edge(side_of):
+        out = jnp.zeros((4, LANES), F32)
+        for i in range(ROWS):
+            moved = jnp.broadcast_to(lateral[i : i + 1, :], (4, LANES))
+            moved = pltpu.roll(moved, (112 + i + side_of) % LANES, 1)
+            out = jnp.where((quarter_lane == 112 + i) & (quarter_row == 2), moved, out)
+        return out
+
+    edge[0, 0] = weight_edge(0)
+    edge[0, 1] = weight_edge(1)
+
     pl.semaphore_wait(barrier, DEVICES - 1)
 
-    def send_group(i, carry):
-        first = (me // 32 + i) % 4 * 4
-
+    places = row_iota((BLOCKS, LANES)) * LANES + lane_iota((BLOCKS, LANES))
+
+    def invert(first, found):
+        for q in range(16):
+            found = jnp.where(places == order_s[first * 16 + q], first * 16 + q, found)
+        return found
+
+    def arrange(first, offset, buffer):
         def order_block(n, c):
             index = jnp.broadcast_to(order[pl.ds(first + n, 1), :], (8, LANES))
-            for k in range(8):
-                ordered[n, k] = pick(fields, k, index)
+            for k in range(4):
+                ordered[n, k] = pick(fields, offset + k, index)
             return c
 
         lax.fori_loop(0, 4, order_block, 0, unroll=4)
-
-        def turn_block(n, c):
-            for j, message in enumerate(swap_pieces([ordered[n, k] for k in range(8)])):
-                send_a[(first + n) * 8 + j] = message
-            return c
-
-        lax.fori_loop(0, 4, turn_block, 0, unroll=4)
-
-        def post(n, c):
-            peer = first * 8 + (me + n) % 32
-            pltpu.make_async_remote_copy(
-                src_ref=send_a.at[peer],
-                dst_ref=recv_a.at[me],
-                send_sem=ring_s.at[0],
-                recv_sem=ring_r.at[0],
-                device_id=place(peer),
-                device_id_type=LOGICAL,
-            ).start()
-            return c
-
-        lax.fori_loop(jnp.where(i == 0, 1, 0), 32, post, 0)
-        return carry
-
-    lax.fori_loop(0, 4, send_group, 0)
-    recv_a[me] = send_a[me]
-
-    places = row_iota((BLOCKS, LANES)) * LANES + lane_iota((BLOCKS, LANES))
-
-    def invert(q, found):
-        return jnp.where(places == order_s[q], q, found)
+        for t in range(2):
+            pack_pair(
+                first // 2 + t,
+                [ordered[2 * t, k] for k in range(4)],
+                [ordered[2 * t + 1, k] for k in range(4)],
+                buffer,
+            )
+
+    def send_group(i, found):
+        first = (me // 32 + i) % 4 * 4
+        arrange(first, 0, send_p)
+
+        def step(n, found):
+            post(0, send_p, recv_p, first * 8 + (me + n) % 32)
+            return invert(i * 32 + n, found)
+
+        return lax.fori_loop(jnp.where(i == 0, 1, 0), 32, step, found)
 
     inverse[...] = lax.fori_loop(
-        0, SOUNDINGS, invert, jnp.zeros((BLOCKS, LANES), jnp.int32), unroll=16
+        0, 4, send_group, invert(0, jnp.zeros((BLOCKS, LANES), jnp.int32))
     )
-
-    run = row_iota((24, LANES))
-    shift = jnp.where(run < 8, 0, jnp.where(run < 16, DEVICES - 1, DEVICES // 2))
-    owner = (me + shift) & (DEVICES - 1)
-    wanted = jnp.where((run & 7) < LINES_DEV, owner * LINES_DEV + (run & 7), -1)
-    for block in range(BLOCKS):
-        hit = line[block : block + 1, :] == wanted
-        onehot[:, block * LANES : (block + 1) * LANES] = jnp.where(hit, 1.0, 0.0)
-    extended[...] = jnp.ones_like(extended)
-    extended[0:LAYERS, :] = model[...]
-
-    def line_sums(slot, values):
-        found = lax.dot_general(
-            onehot[...], values, (((1,), (1,)), ((), ())),
-            precision=lax.Precision.HIGHEST, preferred_element_type=F32,
-        )
-        for g in range(3):
-            sums_s[g, slot, :, 0:PADDED] = found[8 * g : 8 * g + 8, :]
-
-    sums_s[...] = jnp.zeros_like(sums_s)
-    line_sums(0, extended[...])
-    line_sums(1, fields[0:PADDED, :])
-
-    def wait_ring(k, buffer, sem):
-        whole = buffer.at[pl.ds(0, DEVICES - 1)]
-        pltpu.make_async_copy(whole, whole, sem.at[k]).wait()
-
-    wait_ring(0, recv_a, ring_r)
-    wait_ring(0, send_a, ring_s)
-
-    def place_row(i, carry):
-        rows = swap_pieces([recv_a[i * 8 + j] for j in range(8)])
-        for s in range(8):
-            grid[i + 1, s * 8 : s * 8 + 8, :] = rows[s]
-        grid[i + 1, LAYERS : LAYERS + 1, :] = lateral[pl.ds(i, 1), :]
-        return carry
-
-    lax.fori_loop(0, ROWS, place_row, 0, unroll=4)
-
-    lane = lane_iota((PADDED, LANES))
-    layer = row_iota((PADDED, LANES))
-
-    def halo_copies(phase):
+    recv_p[me] = send_p[me]
+
+    def arrange_local(i, c):
+        arrange(i * 4, 4, send_l)
+        return c
+
+    lax.fori_loop(0, 4, arrange_local, 0)
+    recv_l[me] = send_l[me]
+
+    wait_ring(0, recv_p, ring_r)
+
+    def place_pair(pair, c):
+        a, b = unpack_pair(pair, recv_p)
+        for h, rows in ((0, a), (1, b)):
+            i = 2 * pair + h
+            for k in range(4):
+                grid[i + 1, 8 * k : 8 * k + 8, :] = rows[k]
+            grid[i + 1, LAYERS : LAYERS + 1, :] = lateral[pl.ds(i, 1), :]
+        return c
+
+    def halo_start(phase):
         ch = pl.ds(phase * PADDED, PADDED)
         above = (region + REGIONS - 1) % REGIONS * TILES + tile
         below = (region + 1) % REGIONS * TILES + tile
@@ -272,7 +301,7 @@
             (edge.at[phase, 0], side.at[phase, 1], left),
             (edge.at[phase, 1], side.at[phase, 0], right),
         )
-        return [
+        copies = [
             pltpu.make_async_remote_copy(
                 src_ref=src, dst_ref=dst,
                 send_sem=halo_s.at[phase, n], recv_sem=halo_r.at[phase, n],
@@ -280,18 +309,6 @@
             )
             for n, (src, dst, device) in enumerate(pairs)
         ]
-
-    def halo_start(phase):
-        first = phase * PADDED
-        west = jnp.zeros((PADDED, LANES), F32)
-        east = jnp.zeros((PADDED, LANES), F32)
-        for i in range(ROWS):
-            row = grid[i + 1, first : first + PADDED, :]
-            west = jnp.where(lane == i, row if i == 0 else pltpu.roll(row, i, 1), west)
-            east = jnp.where(lane == i, pltpu.roll(row, i + 1, 1), east)
-        edge[phase, 0] = west
-        edge[phase, 1] = east
-        copies = halo_copies(phase)
         for copy in copies:
             copy.start()
         return copies
@@ -311,11 +328,11 @@
 
         @pl.when(tile == 0)
         def _():
-            side[phase, 0] = jnp.zeros((PADDED, LANES), F32)
+            side[phase, 0] = jnp.zeros((4, LANES), F32)
 
         @pl.when(tile == TILES - 1)
         def _():
-            side[phase, 1] = jnp.zeros((PADDED, LANES), F32)
+            side[phase, 1] = jnp.zeros((4, LANES), F32)
 
     def lateral_row(i, phase, west, east):
         ch = slice(phase * PADDED, (phase + 1) * PADDED)
@@ -336,41 +353,55 @@
             + coef[i, 3:4, :] * (here - east_of)
         )
 
+    def side_columns(phase, n, lane_to):
+        twice = jnp.concatenate([side[phase, n], side[phase, n]], axis=0)
+        both = jnp.where(upper, twice, pltpu.roll(twice, 64, 1))
+
+        def column(i):
+            return jnp.concatenate(
+                [pltpu.roll(both, (lane_to - (s * 16 + i)) % LANES, 1) for s in range(4)], axis=0
+            )
+
+        return column
+
     def lateral_part(phase, out):
-        west, east = side[phase, 0], side[phase, 1]
+        west, east = side_columns(phase, 0, 0), side_columns(phase, 1, LANES - 1)
         dots = [zero] * 2
         for i in range(ROWS):
-            west_i = west if i == 0 else pltpu.roll(west, LANES - i, 1)
-            value = lateral_row(i, phase, west_i, pltpu.roll(east, LANES - 1 - i, 1))
+            value = lateral_row(i, phase, west(i), east(i))
             out[i] = value
             if phase == 0:
                 dots[i % 2] = dots[i % 2] + grid[i + 1, 0:PADDED, :] * value
         return dots[0] + dots[1]
 
+    place_pair(0, 0)
+    place_pair(ROWS // 2 - 1, 0)
+    for n in range(2):
+        edge[0, n] = edge[0, n] + edge_of(lambda i: recv_p[i * 8 + 7 * n], n)
     copies = halo_start(0)
+
+    def post_local(n, c):
+        post(3, send_l, recv_l, (me + n) % DEVICES)
+        return c
+
+    lax.fori_loop(1, DEVICES, post_local, 0)
+    lax.fori_loop(1, ROWS // 2 - 1, place_pair, 0, unroll=3)
+
     halo_finish(0, copies)
     lateral_sum = lateral_part(0, c_grid)
 
-    inside = layer < LAYERS
     curve_part = total(jnp.where(inside, lateral_sum + local_sum, 0.0))
     square_part = total(square_sum)
 
-    upper = row_iota((8, LANES)) < 4
-    sublane = row_iota((8, LANES))
-
     def turn_pair(pair):
-        parts = [None] * 8
-        for k in range(4):
-            a = c_grid[2 * pair, 8 * k : 8 * k + 8, :]
-            b = c_grid[2 * pair + 1, 8 * k : 8 * k + 8, :]
-            if k == 3:
-                a = jnp.where(sublane == 6, curve_part, jnp.where(sublane == 7, square_part, a))
-                b = jnp.where(sublane == 6, curve_part, jnp.where(sublane == 7, square_part, b))
-            parts[k] = jnp.where(upper, a, pltpu.roll(b, 4, 0))
-            parts[k + 4] = jnp.where(upper, pltpu.roll(a, 4, 0), b)
-        for j, message in enumerate(swap_pieces(parts)):
-            send_b[pair * 16 + j] = message[0:4]
-            send_b[pair * 16 + 8 + j] = message[4:8]
+        rows = []
+        for h in range(2):
+            row = [c_grid[2 * pair + h, 8 * k : 8 * k + 8, :] for k in range(4)]
+            row[3] = jnp.where(
+                sublane == 6, curve_part, jnp.where(sublane == 7, square_part, row[3])
+            )
+            rows.append(row)
+        pack_pair(pair, rows[0], rows[1], send_b)
 
     def send_half(i, carry):
         first = (me // 64 + i) % 2 * 4
@@ -381,54 +412,72 @@
 
         lax.fori_loop(0, 4, turn, 0, unroll=4)
 
-        def post(n, c):
-            peer = first * 16 + (me + n) % 64
-            pltpu.make_async_remote_copy(
-                src_ref=send_b.at[peer],
-                dst_ref=recv_b.at[me],
-                send_sem=ring_s.at[1],
-                recv_sem=ring_r.at[1],
-                device_id=place(peer),
-                device_id_type=LOGICAL,
-            ).start()
+        def step(n, c):
+            post(1, send_b, recv_b, first * 16 + (me + n) % 64)
             return c
 
-        lax.fori_loop(jnp.where(i == 0, 1, 0), 64, post, 0)
+        lax.fori_loop(jnp.where(i == 0, 1, 0), 64, step, 0)
         return carry
 
     lax.fori_loop(0, 2, send_half, 0)
     recv_b[me] = send_b[me]
 
-    def add_image(i, carry):
-        grid[i + 1, PADDED:, :] = grid[i + 1, PADDED:, :] + c_grid[i]
-        return carry
-
-    lax.fori_loop(0, ROWS, add_image, 0, unroll=4)
+    wait_ring(3, recv_l, ring_r)
+
+    def add_image(pair, c):
+        a, b = unpack_pair(pair, recv_l)
+        for h, rows in ((0, a), (1, b)):
+            i = 2 * pair + h
+            for k in range(4):
+                ch = slice(8 * k, 8 * k + 8)
+                grid[i + 1, PADDED + 8 * k : PADDED + 8 * k + 8, :] = rows[k] + c_grid[i, ch, :]
+        return c
+
+    lax.fori_loop(0, ROWS // 2, add_image, 0, unroll=4)
+    for n in range(2):
+        edge[1, n] = edge_of(lambda i: recv_l[i * 8 + 7 * n] + send_b[i * 8 + 7 * n], n)
     copies = halo_start(1)
+
+    run = row_iota((24, LANES))
+    shift = jnp.where(run < 8, 0, jnp.where(run < 16, DEVICES - 1, DEVICES // 2))
+    owner = (me + shift) & (DEVICES - 1)
+    wanted = jnp.where((run & 7) < LINES_DEV, owner * LINES_DEV + (run & 7), -1)
+    for block in range(BLOCKS):
+        hit = line[block : block + 1, :] == wanted
+        onehot[:, block * LANES : (block + 1) * LANES] = jnp.where(hit, 1.0, 0.0)
+    extended[...] = jnp.ones_like(extended)
+    extended[0:LAYERS, :] = model[...]
+
+    def line_sums(slot, values):
+        found = lax.dot_general(
+            onehot[...], values, (((1,), (1,)), ((), ())),
+            precision=lax.Precision.HIGHEST, preferred_element_type=F32,
+        )
+        for g in range(3):
+            sums_s[g, slot, :, 0:PADDED] = found[8 * g : 8 * g + 8, :]
+
+    sums_s[...] = jnp.zeros_like(sums_s)
+    line_sums(0, extended[...])
+    line_sums(1, fields[0:PADDED, :])
+
     halo_finish(1, copies)
     lateral_part(1, d_grid)
 
     wait_ring(1, recv_b, ring_r)
+    wait_ring(0, send_p, ring_s)
+    wait_ring(3, send_l, ring_s)
     wait_ring(1, send_b, ring_s)
 
-    def unpack_pair(pair, carried):
-        words = [
-            jnp.concatenate([recv_b[pair * 16 + j], recv_b[pair * 16 + 8 + j]], axis=0)
-            for j in range(8)
-        ]
-        parts = swap_pieces(words)
+    def take_pair(pair, carried):
+        a, b = unpack_pair(pair, recv_b)
         even = pl.ds(pl.multiple_of(pair * 2 * LANES, LANES), LANES)
         odd = pl.ds(pl.multiple_of(pair * 2 * LANES + LANES, LANES), LANES)
         for k in range(4):
-            a = jnp.where(upper, parts[k], pltpu.roll(parts[k + 4], 4, 0))
-            b = jnp.where(upper, pltpu.roll(parts[k], 4, 0), parts[k + 4])
-            back[8 * k : 8 * k + 8, even] = a
-            back[8 * k : 8 * k + 8, odd] = b
-            if k == 3:
-                carried = carried + a + b
-        return carried
-
-    carried = lax.fori_loop(0, BLOCKS // 2, unpack_pair, jnp.zeros((8, LANES), F32), unroll=4)
+            back[8 * k : 8 * k + 8, even] = a[k]
+            back[8 * k : 8 * k + 8, odd] = b[k]
+        return carried + a[3] + b[3]
+
+    carried = lax.fori_loop(0, BLOCKS // 2, take_pair, jnp.zeros((8, LANES), F32), unroll=4)
     curve = total(carried[6:7]) * (1.0 / 16)
     square = total(carried[7:8]) * (1.0 / 16)
     step_0 = square / curve
@@ -452,7 +501,7 @@
         )
 
     r_square, r_image, r_curve, r_gates = lax.fori_loop(
-        0, BLOCKS, second_part, (zero, zero, zero, jnp.zeros((GATES, LANES), F32))
+        0, BLOCKS, second_part, (zero, zero, zero, jnp.zeros((GATES, LANES), F32)), unroll=2
     )
 
     def grid_curve(i, acc):
@@ -526,10 +575,15 @@
     profile[...] = means[0:LINES_DEV, 0:LAYERS]
 
 
+def hand_on(model_in, profile_in, model_out, profile_out):
+    model_out[...] = model_in[...]
+    profile_out[...] = profile_in[...]
+
+
 def body(jacobian, misfit, model, vertical_weight, lateral_weight, send_order, line_id):
     vmem = pl.BlockSpec(memory_space=pltpu.VMEM)
     dma = pltpu.SemaphoreType.DMA
-    return pl.pallas_call(
+    outs = pl.pallas_call(
         kernel,
         out_shape=(
             jax.ShapeDtypeStruct((LAYERS, SOUNDINGS), F32),
@@ -548,15 +602,17 @@
             pltpu.VMEM((LAYERS, GATES, SOUNDINGS), jnp.bfloat16),
             pltpu.VMEM((2 * PADDED, SOUNDINGS), F32),
             pltpu.VMEM((PADDED, SOUNDINGS), F32),
-            pltpu.VMEM((4, 8, 8, LANES), F32),
-            pltpu.VMEM((DEVICES, 8, LANES), F32),
-            pltpu.VMEM((DEVICES, 8, LANES), F32),
+            pltpu.VMEM((4, 4, 8, LANES), F32),
+            pltpu.VMEM((DEVICES, 4, LANES), F32),
+            pltpu.VMEM((DEVICES, 4, LANES), F32),
+            pltpu.VMEM((DEVICES, 4, LANES), F32),
+            pltpu.VMEM((DEVICES, 4, LANES), F32),
             pltpu.VMEM((ROWS + 2, 2 * PADDED, LANES), F32),
             pltpu.VMEM((ROWS, 8, LANES), F32),
             pltpu.VMEM((ROWS, PADDED, LANES), F32),
             pltpu.VMEM((ROWS, PADDED, LANES), F32),
-            pltpu.VMEM((2, 2, PADDED, LANES), F32),
-            pltpu.VMEM((2, 2, PADDED, LANES), F32),
+            pltpu.VMEM((2, 2, 4, LANES), F32),
+            pltpu.VMEM((2, 2, 4, LANES), F32),
             pltpu.VMEM((DEVICES, 4, LANES), F32),
             pltpu.VMEM((DEVICES, 4, LANES), F32),
             pltpu.VMEM((PADDED, SOUNDINGS), F32),
@@ -570,8 +626,8 @@
             pltpu.VMEM((DEVICES, 1, LANES), F32),
             dma((7,)),
             dma((CHUNKS,)),
-            dma((3,)),
-            dma((3,)),
+            dma((4,)),
+            dma((4,)),
             dma((2, 4)),
             dma((2, 4)),
             dma((2,)),
@@ -590,6 +646,15 @@
         send_order,
         line_id.reshape(BLOCKS, LANES),
     )
+    return pl.pallas_call(
+        hand_on,
+        out_shape=(
+            jax.ShapeDtypeStruct((LAYERS, SOUNDINGS), F32),
+            jax.ShapeDtypeStruct((LINES_DEV, LAYERS), F32),
+        ),
+        in_specs=[vmem, vmem],
+        out_specs=(vmem, vmem),
+    )(*outs)
 
 
 def solution(mesh):

time: 51 us -> 48.6 us (0.953)
  local copies, waits for them, and re-layouts: 2.92 us -> 0 us
    unnamed x2 -> x0, local copies, waits for them, and re-layouts: 2.92 us -> none
    pallas_call x0 -> x1, Pallas kernels: none -> 1.68 us  [body(): pl.pallas_call(hand_on, out_shape=(jax.ShapeDtypeStruct((LAYERS, SOUNDING...]
    pallas_call x1, Pallas kernels: 47.3 us -> 46.1 us  [body(): pl.pallas_call(kernel, out_shape=(jax.ShapeDtypeStruct((LAYERS, SOUNDINGS...]
where the time goes in v3:
time: 48.6 us; the launch traced here: 48.4 us
  Pallas kernels  47.8 us (98%)
  between operations  0.64 us (1%)
    pallas_call x1, Pallas kernels, body(): pl.pallas_call(kernel, out_shape=(jax.ShapeDtypeStruct((LAYERS, SOUNDINGS...  46.1 us
    pallas_call x1, Pallas kernels, body(): pl.pallas_call(hand_on, out_shape=(jax.ShapeDtypeStruct((LAYERS, SOUNDING...  1.68 us

profile of v3, /device:TPU:1, one launch (start us, length us, event | category | flops | bytes accessed | tf_op | source)
XLA Modules:
  0.0 48.4 jit_solution(3227317233201837447)
XLA Ops:
  0.6 46.1 %shard_map.86 = (f32[30,2048]{1,0:T(8,128)}, f32[4,30]{1,0:T(4,128)}) custom-call(bf16[30,40,2048]{2,1,0:T(8,128)(2,1)} %bitcast.3, f32[40,2048]{1,0:T(8,128)} %misfit_in.1, f32[30,2048]{1,0:T(8,128)} %model_in.1, f32[29,2048]{1,0:T(8,128)} %vertical_in.1, f32[16,128]{1,0:T(8,128)} %lateral_in.1, s32[16,128]{1,0:T(8,128)} %bitcast.4, s32[2048]{0:T(1024)} %order_flat.1, ...), custom_call_target="tpu_custom_call" | custom-call | tf_op jit(solution)/shard_map/pallas_call | solution.py:586
  46.8 1.7 %shard_map.87 = (f32[30,2048]{1,0:T(8,128)}, f32[4,30]{1,0:T(4,128)}) custom-call(f32[30,2048]{1,0:T(8,128)} %get-tuple-element.4.model_in, f32[4,30]{1,0:T(4,128)} %get-tuple-element.5.profile_in), custom_call_target="tpu_custom_call" | custom-call | tf_op jit(solution)/shard_map/pallas_call | solution.py:649

commit v4 on v3

--- a/solution.py
+++ b/solution.py
@@ -231,8 +231,6 @@
     edge[0, 0] = weight_edge(0)
     edge[0, 1] = weight_edge(1)
 
-    pl.semaphore_wait(barrier, DEVICES - 1)
-
     places = row_iota((BLOCKS, LANES)) * LANES + lane_iota((BLOCKS, LANES))
 
     def invert(first, found):
@@ -256,18 +254,20 @@
                 buffer,
             )
 
-    def send_group(i, found):
-        first = (me // 32 + i) % 4 * 4
-        arrange(first, 0, send_p)
-
-        def step(n, found):
-            post(0, send_p, recv_p, first * 8 + (me + n) % 32)
-            return invert(i * 32 + n, found)
-
-        return lax.fori_loop(jnp.where(i == 0, 1, 0), 32, step, found)
+    def arrange_direction(i, c):
+        arrange(i * 4, 0, send_p)
+        return c
+
+    lax.fori_loop(0, 4, arrange_direction, 0)
+
+    pl.semaphore_wait(barrier, DEVICES - 1)
+
+    def post_direction(n, found):
+        post(0, send_p, recv_p, (me + n) % DEVICES)
+        return invert(n, found)
 
     inverse[...] = lax.fori_loop(
-        0, 4, send_group, invert(0, jnp.zeros((BLOCKS, LANES), jnp.int32))
+        1, DEVICES, post_direction, invert(0, jnp.zeros((BLOCKS, LANES), jnp.int32))
     )
     recv_p[me] = send_p[me]
 

time: 48.6 us -> 46.6 us (0.959)
  Pallas kernels: 47.8 us -> 45.9 us
    pallas_call x1, Pallas kernels: 46.1 us -> 44.2 us  [body(): pl.pallas_call(kernel, out_shape=(jax.ShapeDtypeStruct((LAYERS, SOUNDINGS...]
where the time goes in v4:
time: 46.6 us; the launch traced here: 46.5 us
  Pallas kernels  45.9 us (98%)
  between operations  0.64 us (1%)
    pallas_call x1, Pallas kernels, body(): pl.pallas_call(kernel, out_shape=(jax.ShapeDtypeStruct((LAYERS, SOUNDINGS...  44.2 us
    pallas_call x1, Pallas kernels, body(): pl.pallas_call(hand_on, out_shape=(jax.ShapeDtypeStruct((LAYERS, SOUNDING...  1.68 us

profile of v4, /device:TPU:1, one launch (start us, length us, event | category | flops | bytes accessed | tf_op | source)
XLA Modules:
  0.0 46.5 jit_solution(11006026406212783143)
XLA Ops:
  0.6 44.2 %shard_map.86 = (f32[30,2048]{1,0:T(8,128)}, f32[4,30]{1,0:T(4,128)}) custom-call(bf16[30,40,2048]{2,1,0:T(8,128)(2,1)} %bitcast.3, f32[40,2048]{1,0:T(8,128)} %misfit_in.1, f32[30,2048]{1,0:T(8,128)} %model_in.1, f32[29,2048]{1,0:T(8,128)} %vertical_in.1, f32[16,128]{1,0:T(8,128)} %lateral_in.1, s32[16,128]{1,0:T(8,128)} %bitcast.4, s32[2048]{0:T(1024)} %order_flat.1, ...), custom_call_target="tpu_custom_call" | custom-call | tf_op jit(solution)/shard_map/pallas_call | solution.py:586
  44.8 1.7 %shard_map.87 = (f32[30,2048]{1,0:T(8,128)}, f32[4,30]{1,0:T(4,128)}) custom-call(f32[30,2048]{1,0:T(8,128)} %get-tuple-element.4.model_in, f32[4,30]{1,0:T(4,128)} %get-tuple-element.5.profile_in), custom_call_target="tpu_custom_call" | custom-call | tf_op jit(solution)/shard_map/pallas_call | solution.py:649

commit v5 on v4

--- a/solution.py
+++ b/solution.py
@@ -262,13 +262,11 @@
 
     pl.semaphore_wait(barrier, DEVICES - 1)
 
-    def post_direction(n, found):
+    def post_direction(n, c):
         post(0, send_p, recv_p, (me + n) % DEVICES)
-        return invert(n, found)
-
-    inverse[...] = lax.fori_loop(
-        1, DEVICES, post_direction, invert(0, jnp.zeros((BLOCKS, LANES), jnp.int32))
-    )
+        return c
+
+    lax.fori_loop(1, DEVICES, post_direction, 0)
     recv_p[me] = send_p[me]
 
     def arrange_local(i, c):
@@ -460,6 +458,10 @@
     line_sums(0, extended[...])
     line_sums(1, fields[0:PADDED, :])
 
+    inverse[...] = lax.fori_loop(
+        0, SOUNDINGS // 16, invert, jnp.zeros((BLOCKS, LANES), jnp.int32)
+    )
+
     halo_finish(1, copies)
     lateral_part(1, d_grid)
 
@@ -501,7 +503,7 @@
         )
 
     r_square, r_image, r_curve, r_gates = lax.fori_loop(
-        0, BLOCKS, second_part, (zero, zero, zero, jnp.zeros((GATES, LANES), F32)), unroll=2
+        0, BLOCKS, second_part, (zero, zero, zero, jnp.zeros((GATES, LANES), F32)), unroll=4
     )
 
     def grid_curve(i, acc):
@@ -539,8 +541,7 @@
         ).start()
         return carry
 
-    lax.fori_loop(1, DEVICES, share, 0)
-
+    lax.fori_loop(1, 64, share, 0)
     line_sums(2, resid[...])
     sums_copies = []
     for g, offset in ((1, DEVICES - 1), (2, DEVICES // 2)):
@@ -554,6 +555,7 @@
         )
         copy.start()
         sums_copies.append(copy)
+    lax.fori_loop(64, DEVICES, share, 0)
 
     wait_ring(2, part_r, ring_r)
     wait_ring(2, part_r, ring_s)

time: 46.6 us -> 46.1 us (0.989)
  Pallas kernels: 45.9 us -> 45.3 us
    pallas_call x1, Pallas kernels: 44.2 us -> 43.6 us  [body(): pl.pallas_call(kernel, out_shape=(jax.ShapeDtypeStruct((LAYERS, SOUNDINGS...]
where the time goes in v5:
time: 46.1 us; the launch traced here: 45.9 us
  Pallas kernels  45.3 us (98%)
  between operations  0.64 us (1%)
    pallas_call x1, Pallas kernels, body(): pl.pallas_call(kernel, out_shape=(jax.ShapeDtypeStruct((LAYERS, SOUNDINGS...  43.6 us
    pallas_call x1, Pallas kernels, body(): pl.pallas_call(hand_on, out_shape=(jax.ShapeDtypeStruct((LAYERS, SOUNDING...  1.68 us

profile of v5, /device:TPU:1, one launch (start us, length us, event | category | flops | bytes accessed | tf_op | source)
XLA Modules:
  0.0 45.9 jit_solution(10807300580816541967)
XLA Ops:
  0.6 43.6 %shard_map.86 = (f32[30,2048]{1,0:T(8,128)}, f32[4,30]{1,0:T(4,128)}) custom-call(bf16[30,40,2048]{2,1,0:T(8,128)(2,1)} %bitcast.3, f32[40,2048]{1,0:T(8,128)} %misfit_in.1, f32[30,2048]{1,0:T(8,128)} %model_in.1, f32[29,2048]{1,0:T(8,128)} %vertical_in.1, f32[16,128]{1,0:T(8,128)} %lateral_in.1, s32[16,128]{1,0:T(8,128)} %bitcast.4, s32[2048]{0:T(1024)} %order_flat.1, ...), custom_call_target="tpu_custom_call" | custom-call | tf_op jit(solution)/shard_map/pallas_call | solution.py:588
  44.3 1.7 %shard_map.87 = (f32[30,2048]{1,0:T(8,128)}, f32[4,30]{1,0:T(4,128)}) custom-call(f32[30,2048]{1,0:T(8,128)} %get-tuple-element.4.model_in, f32[4,30]{1,0:T(4,128)} %get-tuple-element.5.profile_in), custom_call_target="tpu_custom_call" | custom-call | tf_op jit(solution)/shard_map/pallas_call | solution.py:651

commit v6 on v5

--- a/solution.py
+++ b/solution.py
@@ -136,7 +136,7 @@
         )
         return carry
 
-    lax.fori_loop(1, DEVICES, greet, 0)
+    lax.fori_loop(1, DEVICES, greet, 0, unroll=8)
 
     loads[0].wait()
     loads[1].wait()
@@ -266,7 +266,7 @@
         post(0, send_p, recv_p, (me + n) % DEVICES)
         return c
 
-    lax.fori_loop(1, DEVICES, post_direction, 0)
+    lax.fori_loop(1, DEVICES, post_direction, 0, unroll=8)
     recv_p[me] = send_p[me]
 
     def arrange_local(i, c):
@@ -382,7 +382,7 @@
         post(3, send_l, recv_l, (me + n) % DEVICES)
         return c
 
-    lax.fori_loop(1, DEVICES, post_local, 0)
+    lax.fori_loop(1, DEVICES, post_local, 0, unroll=8)
     lax.fori_loop(1, ROWS // 2 - 1, place_pair, 0, unroll=3)
 
     halo_finish(0, copies)
@@ -541,7 +541,7 @@
         ).start()
         return carry
 
-    lax.fori_loop(1, 64, share, 0)
+    lax.fori_loop(1, 64, share, 0, unroll=8)
     line_sums(2, resid[...])
     sums_copies = []
     for g, offset in ((1, DEVICES - 1), (2, DEVICES // 2)):
@@ -555,7 +555,7 @@
         )
         copy.start()
         sums_copies.append(copy)
-    lax.fori_loop(64, DEVICES, share, 0)
+    lax.fori_loop(64, DEVICES, share, 0, unroll=8)
 
     wait_ring(2, part_r, ring_r)
     wait_ring(2, part_r, ring_s)

time: 46.1 us -> 45.4 us (0.985)
  Pallas kernels: 45.3 us -> 44.7 us
    pallas_call x1, Pallas kernels: 43.6 us -> 43 us  [body(): pl.pallas_call(kernel, out_shape=(jax.ShapeDtypeStruct((LAYERS, SOUNDINGS...]
where the time goes in v6:
time: 45.4 us; the launch traced here: 45.3 us
  Pallas kernels  44.7 us (98%)
  between operations  0.64 us (1%)
    pallas_call x1, Pallas kernels, body(): pl.pallas_call(kernel, out_shape=(jax.ShapeDtypeStruct((LAYERS, SOUNDINGS...  43 us
    pallas_call x1, Pallas kernels, body(): pl.pallas_call(hand_on, out_shape=(jax.ShapeDtypeStruct((LAYERS, SOUNDING...  1.68 us

profile of v6, /device:TPU:1, one launch (start us, length us, event | category | flops | bytes accessed | tf_op | source)
XLA Modules:
  0.0 45.3 jit_solution(16970077167956191094)
XLA Ops:
  0.6 43.0 %shard_map.86 = (f32[30,2048]{1,0:T(8,128)}, f32[4,30]{1,0:T(4,128)}) custom-call(bf16[30,40,2048]{2,1,0:T(8,128)(2,1)} %bitcast.3, f32[40,2048]{1,0:T(8,128)} %misfit_in.1, f32[30,2048]{1,0:T(8,128)} %model_in.1, f32[29,2048]{1,0:T(8,128)} %vertical_in.1, f32[16,128]{1,0:T(8,128)} %lateral_in.1, s32[16,128]{1,0:T(8,128)} %bitcast.4, s32[2048]{0:T(1024)} %order_flat.1, ...), custom_call_target="tpu_custom_call" | custom-call | tf_op jit(solution)/shard_map/pallas_call | solution.py:588
  43.6 1.7 %shard_map.87 = (f32[30,2048]{1,0:T(8,128)}, f32[4,30]{1,0:T(4,128)}) custom-call(f32[30,2048]{1,0:T(8,128)} %get-tuple-element.4.model_in, f32[4,30]{1,0:T(4,128)} %get-tuple-element.5.profile_in), custom_call_target="tpu_custom_call" | custom-call | tf_op jit(solution)/shard_map/pallas_call | solution.py:651

commit v7 on v6

--- a/solution.py
+++ b/solution.py
@@ -276,6 +276,12 @@
     lax.fori_loop(0, 4, arrange_local, 0)
     recv_l[me] = send_l[me]
 
+    def post_local(n, c):
+        post(3, send_l, recv_l, (me + n) % DEVICES)
+        return c
+
+    lax.fori_loop(1, 65, post_local, 0, unroll=8)
+
     wait_ring(0, recv_p, ring_r)
 
     def place_pair(pair, c):
@@ -378,11 +384,7 @@
         edge[0, n] = edge[0, n] + edge_of(lambda i: recv_p[i * 8 + 7 * n], n)
     copies = halo_start(0)
 
-    def post_local(n, c):
-        post(3, send_l, recv_l, (me + n) % DEVICES)
-        return c
-
-    lax.fori_loop(1, DEVICES, post_local, 0, unroll=8)
+    lax.fori_loop(65, DEVICES, post_local, 0, unroll=8)
     lax.fori_loop(1, ROWS // 2 - 1, place_pair, 0, unroll=3)
 
     halo_finish(0, copies)

time: 45.4 us -> 44.9 us (0.989)
  Pallas kernels: 44.7 us -> 44.1 us
    pallas_call x1, Pallas kernels: 43 us -> 42.5 us  [body(): pl.pallas_call(kernel, out_shape=(jax.ShapeDtypeStruct((LAYERS, SOUNDINGS...]
where the time goes in v7:
time: 44.9 us; the launch traced here: 44.8 us
  Pallas kernels  44.1 us (98%)
  between operations  0.64 us (1%)
    pallas_call x1, Pallas kernels, body(): pl.pallas_call(kernel, out_shape=(jax.ShapeDtypeStruct((LAYERS, SOUNDINGS...  42.5 us
    pallas_call x1, Pallas kernels, body(): pl.pallas_call(hand_on, out_shape=(jax.ShapeDtypeStruct((LAYERS, SOUNDING...  1.68 us

profile of v7, /device:TPU:1, one launch (start us, length us, event | category | flops | bytes accessed | tf_op | source)
XLA Modules:
  0.0 44.8 jit_solution(7625503599692449168)
XLA Ops:
  0.6 42.5 %shard_map.86 = (f32[30,2048]{1,0:T(8,128)}, f32[4,30]{1,0:T(4,128)}) custom-call(bf16[30,40,2048]{2,1,0:T(8,128)(2,1)} %bitcast.3, f32[40,2048]{1,0:T(8,128)} %misfit_in.1, f32[30,2048]{1,0:T(8,128)} %model_in.1, f32[29,2048]{1,0:T(8,128)} %vertical_in.1, f32[16,128]{1,0:T(8,128)} %lateral_in.1, s32[16,128]{1,0:T(8,128)} %bitcast.4, s32[2048]{0:T(1024)} %order_flat.1, ...), custom_call_target="tpu_custom_call" | custom-call | tf_op jit(solution)/shard_map/pallas_call | solution.py:590
  43.1 1.7 %shard_map.87 = (f32[30,2048]{1,0:T(8,128)}, f32[4,30]{1,0:T(4,128)}) custom-call(f32[30,2048]{1,0:T(8,128)} %get-tuple-element.4.model_in, f32[4,30]{1,0:T(4,128)} %get-tuple-element.5.profile_in), custom_call_target="tpu_custom_call" | custom-call | tf_op jit(solution)/shard_map/pallas_call | solution.py:653
